TPU v7x, 256 devices: a whole 4x4x8 slice. The times are simulated.
256 devices in a mesh: dp: 64 (over z, y_lo, x), split: 4 (over y_hi, core).
Axes of the slice: x: 4, y: 4 (y_hi: 2, y_lo: 2; y = y_hi * 2 + y_lo), z: 8, core: 2. Of those that a mesh axis runs over, the one named last changes fastest.
Arguments:
- picture_vectors: bfloat16 [16384, 1152], P('dp'), may hold values from -0.59765625 to 0.59765625
- caption_vectors: bfloat16 [16384, 1152], P('dp'), may hold values from -0.59765625 to 0.59765625
- sharpness_entry: float32 [1], replicated, may hold values from 4 to 16
- offset_shift: float32 [1], replicated, may hold values from -4 to -1
Outputs:
- picture_derivative: float32 [16384, 1152], P('dp')
- text_grad: float32 [16384, 1152], P('dp')
- image_loss: float32 [16384], P('dp')
All inputs are finite; a program needn't handle non-finite values.
Results may differ from a plain program's by a relative error of at most 0.0058.
Values may be sent and summed in bfloat16 or wider, within the bound.
A program may use at most 64 MiB of HBM per device.

v0:
```python
import jax
import jax.numpy as jnp
from jax import lax
from jax.sharding import PartitionSpec as P


def passed_along(value, axis, steps):
    count = lax.axis_size(axis)
    pairs = [(source, (source + steps) % count) for source in range(count)]
    return lax.ppermute(value, axis, pairs)


def rescale_to_length(rows):
    values = rows.astype(jnp.float32)
    inverse = lax.rsqrt(jnp.sum(values * values, axis=1, keepdims=True) + 1e-06)
    return (inverse, values * inverse)


def unit_back(unit, inverse, grad):
    return (grad - unit * jnp.sum(unit * grad, axis=1, keepdims=True)) * inverse


def text_move(block, by):
    return passed_along(block, "dp", by)


def grad_move(partial_value, by):
    return passed_along(partial_value, "dp", by)


def per_device(picture_vectors, caption_vectors, sharpness_entry, offset_shift):
    rows = picture_vectors.shape[0]
    nodes = lax.axis_size("dp")
    group_members = lax.axis_size("split")
    place = lax.axis_index("dp")
    group_member = lax.axis_index("split")
    sharpness_factor = sharpness_entry[0]
    offset = offset_shift[0]
    img_inv, image_unit = rescale_to_length(picture_vectors)
    txt_inv, text_unit = rescale_to_length(caption_vectors)
    img_b = image_unit.astype(jnp.bfloat16)
    txt_b = text_unit.astype(jnp.bfloat16)
    diagonal = (
        jnp.arange(rows, dtype=jnp.int32)[:, None] == jnp.arange(rows, dtype=jnp.int32)[None, :]
    )

    def tile(block, owner):
        logits = (
            sharpness_factor
            * lax.dot_general(
                img_b, block, (((1,), (1,)), ((), ())), preferred_element_type=jnp.float32
            )
            + offset
        )
        label = jnp.where(jnp.logical_and(diagonal, owner == place), 1.0, -1.0).astype(jnp.float32)
        pair_loss = jax.nn.softplus(-label * logits)
        coef_b = (-label * jax.nn.sigmoid(-label * logits)).astype(jnp.bfloat16)
        img_part = jnp.dot(coef_b, block, preferred_element_type=jnp.float32)
        text_partial = lax.dot_general(
            coef_b, img_b, (((0,), (0,)), ((), ())), preferred_element_type=jnp.float32
        )
        return (img_part, text_partial, jnp.sum(pair_loss, axis=1))

    current = txt_b
    for step in range(group_members - 1):
        moved = passed_along(current, "dp", 1)
        current = jnp.where(group_member > step, moved, current)
    owner = (place - group_member) % nodes
    zeros = jnp.zeros((rows, txt_b.shape[1]), jnp.float32)
    img_acc = zeros
    loss_acc = jnp.zeros((rows,), jnp.float32)
    steps = nodes // group_members

    def one_way(state, unused):
        block, block_owner, txt_sum, img_sum, loss_running_sum = state
        img_one, txt_one, loss_one = tile(block, block_owner)
        txt_sum = grad_move(txt_sum + txt_one, group_members)
        block = text_move(block, group_members)
        state = (
            block,
            (block_owner - group_members) % nodes,
            txt_sum,
            img_sum + img_one,
            loss_running_sum + loss_one,
        )
        return (state, None)

    final, unused = lax.scan(
        one_way, (current, owner, zeros, img_acc, loss_acc), None, length=steps
    )
    text_accumulator, img_acc, loss_acc = (final[2], final[3], final[4])
    for step in range(group_members - 1):
        moved = passed_along(text_accumulator, "dp", -1)
        text_accumulator = jnp.where(group_member > step, moved, text_accumulator)
    picture_aggregate, text_grand_total, loss_total = lax.psum(
        (img_acc, text_accumulator, loss_acc), "split"
    )
    picture_derivative = unit_back(image_unit, img_inv, sharpness_factor * picture_aggregate)
    text_grad = unit_back(text_unit, txt_inv, sharpness_factor * text_grand_total)
    image_loss = loss_total / (rows * nodes)
    return (picture_derivative, text_grad, image_loss)


def solution(mesh):
    placed = (P("dp", None), P("dp", None), P(), P())
    return jax.shard_map(
        per_device,
        mesh=mesh,
        in_specs=placed,
        out_specs=(P("dp", None), P("dp", None), P("dp")),
        check_vma=False,
    )
```

profile of v0, /device:TPU:1, one launch (start us, length us, event | category | flops | bytes accessed | tf_op | source)
XLA Modules:
  0.0 891.1 jit_solution(5331846693622849512)
XLA Ops:
  11.9 20.6 %collective-permute-done.2 = bf16[256,1152]{1,0:T(8,128)(2,1)S(1)} collective-permute-done((bf16[256,1152]{1,0:T(8,128)(2,1)S(1)}, bf16[256,1152]{1,0:T(8,128)(2,1)S(1)}, u32[]{:S(2)}, u32[]{:S(2)}) %collective-permute-start.2) | collective-permute-done | bytes 589856 | tf_op jit(solution)/shard_map/ppermute | solution.py:10
  33.1 17.6 %collective-permute-done.3 = bf16[256,1152]{1,0:T(8,128)(2,1)S(1)} collective-permute-done((bf16[256,1152]{1,0:T(8,128)(2,1)S(1)}, bf16[256,1152]{1,0:T(8,128)(2,1)S(1)}, u32[]{:S(2)}, u32[]{:S(2)}) %collective-permute-start.3) | collective-permute-done | bytes 589856 | tf_op jit(solution)/shard_map/ppermute | solution.py:10
  51.9 15.8 %collective-permute-done.4 = bf16[256,1152]{1,0:T(8,128)(2,1)S(1)} collective-permute-done((bf16[256,1152]{1,0:T(8,128)(2,1)S(1)}, bf16[256,1152]{1,0:T(8,128)(2,1)S(1)}, u32[]{:S(2)}, u32[]{:S(2)}) %collective-permute-start.4) | collective-permute-done | bytes 589856 | tf_op jit(solution)/shard_map/ppermute | solution.py:10
  68.7 636.0 %while.21 = (s32[]{:T(128)}, bf16[256,1152]{1,0:T(8,128)(2,1)}, s32[]{:T(128)}, f32[256,1152]{1,0:T(8,128)S(1)}, f32[256,1152]{1,0:T(8,128)S(1)}, /*index=5*/f32...) while((s32[]{:T(128)}, bf16[256,1152]{1,0:T(8,128)(2,1)}, ...), condition=%wide.region_4.5_spmd.clone, body=%wide.region_2.4_spmd.clone.sunk | while | flops 455966976 | bytes 16126325 | solution.py:88
  75.8 38.7 %collective-permute-done = bf16[256,1152]{1,0:T(8,128)(2,1)} collective-permute-done((bf16[256,1152]{1,0:T(8,128)(2,1)S(1)}, bf16[256,1152]{1,0:T(8,128)(2,1)}, u32[]{:S(2)}, u32[]{:S(2)}) %collective-permute-start) | collective-permute-done | bytes 589856 | tf_op jit(solution)/shard_map/while/body/eval_jaxpr/ppermute | solution.py:10
  121.7 37.8 %collective-permute-done = bf16[256,1152]{1,0:T(8,128)(2,1)} collective-permute-done((bf16[256,1152]{1,0:T(8,128)(2,1)S(1)}, bf16[256,1152]{1,0:T(8,128)(2,1)}, u32[]{:S(2)}, u32[]{:S(2)}) %collective-permute-start) | collective-permute-done | bytes 589856 | tf_op jit(solution)/shard_map/while/body/eval_jaxpr/ppermute | solution.py:10
  166.6 36.9 %collective-permute-done = bf16[256,1152]{1,0:T(8,128)(2,1)} collective-permute-done((bf16[256,1152]{1,0:T(8,128)(2,1)S(1)}, bf16[256,1152]{1,0:T(8,128)(2,1)}, u32[]{:S(2)}, u32[]{:S(2)}) %collective-permute-start) | collective-permute-done | bytes 589856 | tf_op jit(solution)/shard_map/while/body/eval_jaxpr/ppermute | solution.py:10
  210.6 35.8 %collective-permute-done = bf16[256,1152]{1,0:T(8,128)(2,1)} collective-permute-done((bf16[256,1152]{1,0:T(8,128)(2,1)S(1)}, bf16[256,1152]{1,0:T(8,128)(2,1)}, u32[]{:S(2)}, u32[]{:S(2)}) %collective-permute-start) | collective-permute-done | bytes 589856 | tf_op jit(solution)/shard_map/while/body/eval_jaxpr/ppermute | solution.py:10
  253.6 34.8 %collective-permute-done = bf16[256,1152]{1,0:T(8,128)(2,1)} collective-permute-done((bf16[256,1152]{1,0:T(8,128)(2,1)S(1)}, bf16[256,1152]{1,0:T(8,128)(2,1)}, u32[]{:S(2)}, u32[]{:S(2)}) %collective-permute-start) | collective-permute-done | bytes 589856 | tf_op jit(solution)/shard_map/while/body/eval_jaxpr/ppermute | solution.py:10
  295.6 33.8 %collective-permute-done = bf16[256,1152]{1,0:T(8,128)(2,1)} collective-permute-done((bf16[256,1152]{1,0:T(8,128)(2,1)S(1)}, bf16[256,1152]{1,0:T(8,128)(2,1)}, u32[]{:S(2)}, u32[]{:S(2)}) %collective-permute-start) | collective-permute-done | bytes 589856 | tf_op jit(solution)/shard_map/while/body/eval_jaxpr/ppermute | solution.py:10
  336.5 32.7 %collective-permute-done = bf16[256,1152]{1,0:T(8,128)(2,1)} collective-permute-done((bf16[256,1152]{1,0:T(8,128)(2,1)S(1)}, bf16[256,1152]{1,0:T(8,128)(2,1)}, u32[]{:S(2)}, u32[]{:S(2)}) %collective-permute-start) | collective-permute-done | bytes 589856 | tf_op jit(solution)/shard_map/while/body/eval_jaxpr/ppermute | solution.py:10
  376.4 31.7 %collective-permute-done = bf16[256,1152]{1,0:T(8,128)(2,1)} collective-permute-done((bf16[256,1152]{1,0:T(8,128)(2,1)S(1)}, bf16[256,1152]{1,0:T(8,128)(2,1)}, u32[]{:S(2)}, u32[]{:S(2)}) %collective-permute-start) | collective-permute-done | bytes 589856 | tf_op jit(solution)/shard_map/while/body/eval_jaxpr/ppermute | solution.py:10
  415.3 30.7 %collective-permute-done = bf16[256,1152]{1,0:T(8,128)(2,1)} collective-permute-done((bf16[256,1152]{1,0:T(8,128)(2,1)S(1)}, bf16[256,1152]{1,0:T(8,128)(2,1)}, u32[]{:S(2)}, u32[]{:S(2)}) %collective-permute-start) | collective-permute-done | bytes 589856 | tf_op jit(solution)/shard_map/while/body/eval_jaxpr/ppermute | solution.py:10
  453.1 29.8 %collective-permute-done = bf16[256,1152]{1,0:T(8,128)(2,1)} collective-permute-done((bf16[256,1152]{1,0:T(8,128)(2,1)S(1)}, bf16[256,1152]{1,0:T(8,128)(2,1)}, u32[]{:S(2)}, u32[]{:S(2)}) %collective-permute-start) | collective-permute-done | bytes 589856 | tf_op jit(solution)/shard_map/while/body/eval_jaxpr/ppermute | solution.py:10
  490.1 29.8 %collective-permute-done = bf16[256,1152]{1,0:T(8,128)(2,1)} collective-permute-done((bf16[256,1152]{1,0:T(8,128)(2,1)S(1)}, bf16[256,1152]{1,0:T(8,128)(2,1)}, u32[]{:S(2)}, u32[]{:S(2)}) %collective-permute-start) | collective-permute-done | bytes 589856 | tf_op jit(solution)/shard_map/while/body/eval_jaxpr/ppermute | solution.py:10
  527.0 29.8 %collective-permute-done = bf16[256,1152]{1,0:T(8,128)(2,1)} collective-permute-done((bf16[256,1152]{1,0:T(8,128)(2,1)S(1)}, bf16[256,1152]{1,0:T(8,128)(2,1)}, u32[]{:S(2)}, u32[]{:S(2)}) %collective-permute-start) | collective-permute-done | bytes 589856 | tf_op jit(solution)/shard_map/while/body/eval_jaxpr/ppermute | solution.py:10
  564.0 29.8 %collective-permute-done = bf16[256,1152]{1,0:T(8,128)(2,1)} collective-permute-done((bf16[256,1152]{1,0:T(8,128)(2,1)S(1)}, bf16[256,1152]{1,0:T(8,128)(2,1)}, u32[]{:S(2)}, u32[]{:S(2)}) %collective-permute-start) | collective-permute-done | bytes 589856 | tf_op jit(solution)/shard_map/while/body/eval_jaxpr/ppermute | solution.py:10
  600.9 29.8 %collective-permute-done = bf16[256,1152]{1,0:T(8,128)(2,1)} collective-permute-done((bf16[256,1152]{1,0:T(8,128)(2,1)S(1)}, bf16[256,1152]{1,0:T(8,128)(2,1)}, u32[]{:S(2)}, u32[]{:S(2)}) %collective-permute-start) | collective-permute-done | bytes 589856 | tf_op jit(solution)/shard_map/while/body/eval_jaxpr/ppermute | solution.py:10
  637.9 29.8 %collective-permute-done = bf16[256,1152]{1,0:T(8,128)(2,1)} collective-permute-done((bf16[256,1152]{1,0:T(8,128)(2,1)S(1)}, bf16[256,1152]{1,0:T(8,128)(2,1)}, u32[]{:S(2)}, u32[]{:S(2)}) %collective-permute-start) | collective-permute-done | bytes 589856 | tf_op jit(solution)/shard_map/while/body/eval_jaxpr/ppermute | solution.py:10
  674.9 29.8 %collective-permute-done = bf16[256,1152]{1,0:T(8,128)(2,1)} collective-permute-done((bf16[256,1152]{1,0:T(8,128)(2,1)S(1)}, bf16[256,1152]{1,0:T(8,128)(2,1)}, u32[]{:S(2)}, u32[]{:S(2)}) %collective-permute-start) | collective-permute-done | bytes 589856 | tf_op jit(solution)/shard_map/while/body/eval_jaxpr/ppermute | solution.py:10
  724.3 20.5 %collective-permute-done.6 = f32[256,1152]{1,0:T(8,128)S(1)} collective-permute-done((f32[256,1152]{1,0:T(8,128)S(1)}, f32[256,1152]{1,0:T(8,128)S(1)}, u32[]{:S(2)}, u32[]{:S(2)}) %collective-permute-start.6) | collective-permute-done | bytes 1179680 | tf_op jit(solution)/shard_map/ppermute | solution.py:10
  745.0 25.5 %collective-permute-done.7 = f32[256,1152]{1,0:T(8,128)S(1)} collective-permute-done((f32[256,1152]{1,0:T(8,128)S(1)}, f32[256,1152]{1,0:T(8,128)S(1)}, u32[]{:S(2)}, u32[]{:S(2)}) %collective-permute-start.7) | collective-permute-done | bytes 1179680 | tf_op jit(solution)/shard_map/ppermute | solution.py:10
  772.4 48.5 %psum.23 = f32[256]{0:T(256)S(1)} all-reduce(f32[256]{0:T(256)S(1)} %get-tuple-element.146), channel_id=1, replica_groups=mesh['dp'=64,'split'=4] {'split'}, use_global_device_ids=true, to_apply=%region_9.10 | all-reduce | flops 256 | bytes 2048 | tf_op jit(solution)/shard_map/psum | solution.py:95
  821.4 58.0 %all-reduce.3.cloned.1.call-done = (f32[256,1152]{1,0:T(8,128)}, f32[256,1152]{1,0:T(8,128)}) async-done(((f32[256,1152]{1,0:T(8,128)}, f32[256,1152]{1,0:T(8,128)}), (f32[256,1152]{1,0:T(8,128)}, f32[256,1152]{1,0:T(8,128)})) %all-reduce.3.cloned.1.call-update) | async-done | bytes 2359312 | tf_op jit(solution)/shard_map/psum | solution.py:95
  (170 shorter events, 148.1 us)
Async XLA Ops:
  7.2 872.3 %all-reduce.3.cloned.1.call-start = ((), (), s32[]{:S(2)}) async-start(), calls=%async_computation | async-start | bytes 4718592 | tf_op jit(solution)/shard_map/psum | solution.py:95
  75.1 39.5 %collective-permute-start.1 = (f32[256,1152]{1,0:T(8,128)}, f32[256,1152]{1,0:T(8,128)S(1)}, u32[]{:S(2)}, u32[]{:S(2)}) collective-permute-start(f32[256,1152]{1,0:T(8,128)} %convolution_add_fusion.4), channel_id=1, source_target_pairs={{0,16},{4,20},{8,24},{12,28},{16,32},{20,36},{24,40},{28,44},{32,4... | collective-permute-start | bytes 3538952 | tf_op jit(solution)/shard_map/while/body/eval_jaxpr/ppermute | solution.py:10
  75.1 39.5 %collective-permute-start = (bf16[256,1152]{1,0:T(8,128)(2,1)S(1)}, bf16[256,1152]{1,0:T(8,128)(2,1)}, u32[]{:S(2)}, u32[]{:S(2)}) collective-permute-start(bf16[256,1152]{1,0:T(8,128)(2,1)S(1)} %copy.14), channel_id=1, source_target_pairs={{0,16},{4,20},{8,24},{12,28},{16,32},{20,36},{24,40},{28,44},{32,4... | collective-permute-start | bytes 1769480 | tf_op jit(solution)/shard_map/while/body/eval_jaxpr/ppermute | solution.py:10
  120.9 38.5 %collective-permute-start.1 = (f32[256,1152]{1,0:T(8,128)}, f32[256,1152]{1,0:T(8,128)S(1)}, u32[]{:S(2)}, u32[]{:S(2)}) collective-permute-start(f32[256,1152]{1,0:T(8,128)} %convolution_add_fusion.4), channel_id=1, source_target_pairs={{0,16},{4,20},{8,24},{12,28},{16,32},{20,36},{24,40},{28,44},{32,4... | collective-permute-start | bytes 3538952 | tf_op jit(solution)/shard_map/while/body/eval_jaxpr/ppermute | solution.py:10
  120.9 38.5 %collective-permute-start = (bf16[256,1152]{1,0:T(8,128)(2,1)S(1)}, bf16[256,1152]{1,0:T(8,128)(2,1)}, u32[]{:S(2)}, u32[]{:S(2)}) collective-permute-start(bf16[256,1152]{1,0:T(8,128)(2,1)S(1)} %copy.14), channel_id=1, source_target_pairs={{0,16},{4,20},{8,24},{12,28},{16,32},{20,36},{24,40},{28,44},{32,4... | collective-permute-start | bytes 1769480 | tf_op jit(solution)/shard_map/while/body/eval_jaxpr/ppermute | solution.py:10
  165.9 37.6 %collective-permute-start.1 = (f32[256,1152]{1,0:T(8,128)}, f32[256,1152]{1,0:T(8,128)S(1)}, u32[]{:S(2)}, u32[]{:S(2)}) collective-permute-start(f32[256,1152]{1,0:T(8,128)} %convolution_add_fusion.4), channel_id=1, source_target_pairs={{0,16},{4,20},{8,24},{12,28},{16,32},{20,36},{24,40},{28,44},{32,4... | collective-permute-start | bytes 3538952 | tf_op jit(solution)/shard_map/while/body/eval_jaxpr/ppermute | solution.py:10
  165.9 37.6 %collective-permute-start = (bf16[256,1152]{1,0:T(8,128)(2,1)S(1)}, bf16[256,1152]{1,0:T(8,128)(2,1)}, u32[]{:S(2)}, u32[]{:S(2)}) collective-permute-start(bf16[256,1152]{1,0:T(8,128)(2,1)S(1)} %copy.14), channel_id=1, source_target_pairs={{0,16},{4,20},{8,24},{12,28},{16,32},{20,36},{24,40},{28,44},{32,4... | collective-permute-start | bytes 1769480 | tf_op jit(solution)/shard_map/while/body/eval_jaxpr/ppermute | solution.py:10
  209.9 36.6 %collective-permute-start.1 = (f32[256,1152]{1,0:T(8,128)}, f32[256,1152]{1,0:T(8,128)S(1)}, u32[]{:S(2)}, u32[]{:S(2)}) collective-permute-start(f32[256,1152]{1,0:T(8,128)} %convolution_add_fusion.4), channel_id=1, source_target_pairs={{0,16},{4,20},{8,24},{12,28},{16,32},{20,36},{24,40},{28,44},{32,4... | collective-permute-start | bytes 3538952 | tf_op jit(solution)/shard_map/while/body/eval_jaxpr/ppermute | solution.py:10
  209.9 36.6 %collective-permute-start = (bf16[256,1152]{1,0:T(8,128)(2,1)S(1)}, bf16[256,1152]{1,0:T(8,128)(2,1)}, u32[]{:S(2)}, u32[]{:S(2)}) collective-permute-start(bf16[256,1152]{1,0:T(8,128)(2,1)S(1)} %copy.14), channel_id=1, source_target_pairs={{0,16},{4,20},{8,24},{12,28},{16,32},{20,36},{24,40},{28,44},{32,4... | collective-permute-start | bytes 1769480 | tf_op jit(solution)/shard_map/while/body/eval_jaxpr/ppermute | solution.py:10
  252.9 35.6 %collective-permute-start.1 = (f32[256,1152]{1,0:T(8,128)}, f32[256,1152]{1,0:T(8,128)S(1)}, u32[]{:S(2)}, u32[]{:S(2)}) collective-permute-start(f32[256,1152]{1,0:T(8,128)} %convolution_add_fusion.4), channel_id=1, source_target_pairs={{0,16},{4,20},{8,24},{12,28},{16,32},{20,36},{24,40},{28,44},{32,4... | collective-permute-start | bytes 3538952 | tf_op jit(solution)/shard_map/while/body/eval_jaxpr/ppermute | solution.py:10
  252.9 35.6 %collective-permute-start = (bf16[256,1152]{1,0:T(8,128)(2,1)S(1)}, bf16[256,1152]{1,0:T(8,128)(2,1)}, u32[]{:S(2)}, u32[]{:S(2)}) collective-permute-start(bf16[256,1152]{1,0:T(8,128)(2,1)S(1)} %copy.14), channel_id=1, source_target_pairs={{0,16},{4,20},{8,24},{12,28},{16,32},{20,36},{24,40},{28,44},{32,4... | collective-permute-start | bytes 1769480 | tf_op jit(solution)/shard_map/while/body/eval_jaxpr/ppermute | solution.py:10
  294.8 34.5 %collective-permute-start.1 = (f32[256,1152]{1,0:T(8,128)}, f32[256,1152]{1,0:T(8,128)S(1)}, u32[]{:S(2)}, u32[]{:S(2)}) collective-permute-start(f32[256,1152]{1,0:T(8,128)} %convolution_add_fusion.4), channel_id=1, source_target_pairs={{0,16},{4,20},{8,24},{12,28},{16,32},{20,36},{24,40},{28,44},{32,4... | collective-permute-start | bytes 3538952 | tf_op jit(solution)/shard_map/while/body/eval_jaxpr/ppermute | solution.py:10
  294.8 34.5 %collective-permute-start = (bf16[256,1152]{1,0:T(8,128)(2,1)S(1)}, bf16[256,1152]{1,0:T(8,128)(2,1)}, u32[]{:S(2)}, u32[]{:S(2)}) collective-permute-start(bf16[256,1152]{1,0:T(8,128)(2,1)S(1)} %copy.14), channel_id=1, source_target_pairs={{0,16},{4,20},{8,24},{12,28},{16,32},{20,36},{24,40},{28,44},{32,4... | collective-permute-start | bytes 1769480 | tf_op jit(solution)/shard_map/while/body/eval_jaxpr/ppermute | solution.py:10
  335.8 33.5 %collective-permute-start.1 = (f32[256,1152]{1,0:T(8,128)}, f32[256,1152]{1,0:T(8,128)S(1)}, u32[]{:S(2)}, u32[]{:S(2)}) collective-permute-start(f32[256,1152]{1,0:T(8,128)} %convolution_add_fusion.4), channel_id=1, source_target_pairs={{0,16},{4,20},{8,24},{12,28},{16,32},{20,36},{24,40},{28,44},{32,4... | collective-permute-start | bytes 3538952 | tf_op jit(solution)/shard_map/while/body/eval_jaxpr/ppermute | solution.py:10
  335.8 33.5 %collective-permute-start = (bf16[256,1152]{1,0:T(8,128)(2,1)S(1)}, bf16[256,1152]{1,0:T(8,128)(2,1)}, u32[]{:S(2)}, u32[]{:S(2)}) collective-permute-start(bf16[256,1152]{1,0:T(8,128)(2,1)S(1)} %copy.14), channel_id=1, source_target_pairs={{0,16},{4,20},{8,24},{12,28},{16,32},{20,36},{24,40},{28,44},{32,4... | collective-permute-start | bytes 1769480 | tf_op jit(solution)/shard_map/while/body/eval_jaxpr/ppermute | solution.py:10
  375.7 32.5 %collective-permute-start.1 = (f32[256,1152]{1,0:T(8,128)}, f32[256,1152]{1,0:T(8,128)S(1)}, u32[]{:S(2)}, u32[]{:S(2)}) collective-permute-start(f32[256,1152]{1,0:T(8,128)} %convolution_add_fusion.4), channel_id=1, source_target_pairs={{0,16},{4,20},{8,24},{12,28},{16,32},{20,36},{24,40},{28,44},{32,4... | collective-permute-start | bytes 3538952 | tf_op jit(solution)/shard_map/while/body/eval_jaxpr/ppermute | solution.py:10
  375.7 32.5 %collective-permute-start = (bf16[256,1152]{1,0:T(8,128)(2,1)S(1)}, bf16[256,1152]{1,0:T(8,128)(2,1)}, u32[]{:S(2)}, u32[]{:S(2)}) collective-permute-start(bf16[256,1152]{1,0:T(8,128)(2,1)S(1)} %copy.14), channel_id=1, source_target_pairs={{0,16},{4,20},{8,24},{12,28},{16,32},{20,36},{24,40},{28,44},{32,4... | collective-permute-start | bytes 1769480 | tf_op jit(solution)/shard_map/while/body/eval_jaxpr/ppermute | solution.py:10
  414.5 31.5 %collective-permute-start.1 = (f32[256,1152]{1,0:T(8,128)}, f32[256,1152]{1,0:T(8,128)S(1)}, u32[]{:S(2)}, u32[]{:S(2)}) collective-permute-start(f32[256,1152]{1,0:T(8,128)} %convolution_add_fusion.4), channel_id=1, source_target_pairs={{0,16},{4,20},{8,24},{12,28},{16,32},{20,36},{24,40},{28,44},{32,4... | collective-permute-start | bytes 3538952 | tf_op jit(solution)/shard_map/while/body/eval_jaxpr/ppermute | solution.py:10
  414.5 31.4 %collective-permute-start = (bf16[256,1152]{1,0:T(8,128)(2,1)S(1)}, bf16[256,1152]{1,0:T(8,128)(2,1)}, u32[]{:S(2)}, u32[]{:S(2)}) collective-permute-start(bf16[256,1152]{1,0:T(8,128)(2,1)S(1)} %copy.14), channel_id=1, source_target_pairs={{0,16},{4,20},{8,24},{12,28},{16,32},{20,36},{24,40},{28,44},{32,4... | collective-permute-start | bytes 1769480 | tf_op jit(solution)/shard_map/while/body/eval_jaxpr/ppermute | solution.py:10
  489.3 30.6 %collective-permute-start.1 = (f32[256,1152]{1,0:T(8,128)}, f32[256,1152]{1,0:T(8,128)S(1)}, u32[]{:S(2)}, u32[]{:S(2)}) collective-permute-start(f32[256,1152]{1,0:T(8,128)} %convolution_add_fusion.4), channel_id=1, source_target_pairs={{0,16},{4,20},{8,24},{12,28},{16,32},{20,36},{24,40},{28,44},{32,4... | collective-permute-start | bytes 3538952 | tf_op jit(solution)/shard_map/while/body/eval_jaxpr/ppermute | solution.py:10
  526.3 30.6 %collective-permute-start.1 = (f32[256,1152]{1,0:T(8,128)}, f32[256,1152]{1,0:T(8,128)S(1)}, u32[]{:S(2)}, u32[]{:S(2)}) collective-permute-start(f32[256,1152]{1,0:T(8,128)} %convolution_add_fusion.4), channel_id=1, source_target_pairs={{0,16},{4,20},{8,24},{12,28},{16,32},{20,36},{24,40},{28,44},{32,4... | collective-permute-start | bytes 3538952 | tf_op jit(solution)/shard_map/while/body/eval_jaxpr/ppermute | solution.py:10
  563.2 30.6 %collective-permute-start.1 = (f32[256,1152]{1,0:T(8,128)}, f32[256,1152]{1,0:T(8,128)S(1)}, u32[]{:S(2)}, u32[]{:S(2)}) collective-permute-start(f32[256,1152]{1,0:T(8,128)} %convolution_add_fusion.4), channel_id=1, source_target_pairs={{0,16},{4,20},{8,24},{12,28},{16,32},{20,36},{24,40},{28,44},{32,4... | collective-permute-start | bytes 3538952 | tf_op jit(solution)/shard_map/while/body/eval_jaxpr/ppermute | solution.py:10
  563.2 30.6 %collective-permute-start = (bf16[256,1152]{1,0:T(8,128)(2,1)S(1)}, bf16[256,1152]{1,0:T(8,128)(2,1)}, u32[]{:S(2)}, u32[]{:S(2)}) collective-permute-start(bf16[256,1152]{1,0:T(8,128)(2,1)S(1)} %copy.14), channel_id=1, source_target_pairs={{0,16},{4,20},{8,24},{12,28},{16,32},{20,36},{24,40},{28,44},{32,4... | collective-permute-start | bytes 1769480 | tf_op jit(solution)/shard_map/while/body/eval_jaxpr/ppermute | solution.py:10
  600.2 30.6 %collective-permute-start.1 = (f32[256,1152]{1,0:T(8,128)}, f32[256,1152]{1,0:T(8,128)S(1)}, u32[]{:S(2)}, u32[]{:S(2)}) collective-permute-start(f32[256,1152]{1,0:T(8,128)} %convolution_add_fusion.4), channel_id=1, source_target_pairs={{0,16},{4,20},{8,24},{12,28},{16,32},{20,36},{24,40},{28,44},{32,4... | collective-permute-start | bytes 3538952 | tf_op jit(solution)/shard_map/while/body/eval_jaxpr/ppermute | solution.py:10
  (22 other events, 681.4 us)
Sparse Core Ops, SparseCore 0:
  771.8 107.6 all-reduce.2
where the time goes:
time: 894 us; the launch traced here: 891 us
  waiting for transfers between devices  695 us (78%)
  matrix products  97 us (11%)
  blocking collectives  48.5 us (5%)
  local copies, waits for them, and re-layouts  17.2 us (2%)
  between operations  14.9 us (2%)
  other arithmetic  11.9 us (1%)
    ppermute x38, waiting for transfers between devices, passed_along(): return lax.ppermute(value, axis, pairs)  637 us
    psum x1, waiting for transfers between devices, per_device(): lax.psum((img_acc, text_accumulator, loss_acc), 'split')  58 us
    psum x1, blocking collectives, per_device(): lax.psum((img_acc, text_accumulator, loss_acc), 'split')  48.5 us
    dot_general x16, matrix products, tile(): lax.dot_general(img_b, block, (((1,), (1,)), ((), ())), preferred_element...  46.1 us
    dot_general x16, matrix products, tile(): lax.dot_general(coef_b, img_b, (((0,), (0,)), ((), ())), preferred_elemen...  39.1 us
  transfers between devices with their start and end apart: 39, of which 23 were waited for; matrix products, arithmetic and copies ran while one was open for 2% of the time, Pallas kernels for 0%

commit v1 on v0

v1 whole, which is shorter than its diff:
```python
import jax
import jax.numpy as jnp
from jax import lax
from jax.experimental import pallas as pl
from jax.experimental.pallas import tpu as pltpu
from jax.sharding import PartitionSpec as P

MESH = pl.DeviceIdType.MESH
F32 = jnp.float32
BF16 = jnp.bfloat16

NX, NY, NZ = 4, 4, 8
ROWS, WIDTH = 256, 1152
HALF, QUARTER, EIGHTH = 128, 64, 32
PAIRS = 16384


def unit_rows(values):
    values = values.astype(F32)
    inverse = lax.rsqrt(jnp.sum(values * values, axis=1, keepdims=True) + 1e-06)
    return inverse, values * inverse


def unit_back(unit, inverse, grad):
    return (grad - unit * jnp.sum(unit * grad, axis=1, keepdims=True)) * inverse


def contract(a, b, dims):
    return lax.dot_general(a, b, (dims, ((), ())), preferred_element_type=F32)


def kernel(
    pic_hbm, cap_hbm, sharp_ref, off_ref,
    img_out, txt_out, loss_out,
    pic, cap, ibuf, jbuf, cbuf, ctbuf, pacc, tacc, lacc,
    pb, xr1, x2, rb, qr,
    ts, tr, vs, vr,
    ls, lx, rl, lq,
    hop,
    in_sem, i_s, i_r, t_s, t_r, d_s, d_r, x1_s, x1_r, x2_s, x2_r, y_s, y_r,
    ly_s, ly_r, lx_s, lx_r, e_s, e_r, v_s, v_r, g_s, g_r,
):
    dp, split = lax.axis_index("dp"), lax.axis_index("split")
    x = lax.rem(dp, NX)
    yl = lax.rem(dp // NX, 2)
    z = dp // (2 * NX)
    yh, core = split // 2, lax.rem(split, 2)
    y = 2 * yh + yl
    other = 1 - core
    first = core == 0
    second = core == 1

    def at(px, py, pz, pc):
        px, py, pz = lax.rem(px, NX), lax.rem(py, NY), lax.rem(pz, NZ)
        return ((pz * 2 + lax.rem(py, 2)) * NX + px, (py // 2) * 2 + pc)

    sibling = at(x, y, z, other)
    x_up, x_down, x_far = (at(x + k, y, z, core) for k in (1, 3, 2))
    z_up, z_down = at(x, y, z + 1, core), at(x, y, z + 7, core)
    y_up1, y_down1 = at(x, y + 1, z, 1), at(x, y + 3, z, 1)

    own_text = pl.multiple_of(yh * HALF, HALF)
    fetch_text = pltpu.make_async_copy(cap_hbm.at[pl.ds(own_text, HALF)], cap, in_sem.at[0])
    fetch_image = pltpu.make_async_copy(pic_hbm, pic, in_sem.at[1])
    fetch_text.start()
    fetch_image.start()

    barrier = pltpu.get_barrier_semaphore()
    partners = [sibling, x_up, x_down, x_far, z_up, z_down]
    partners += [at(x, y + k, z, c) for k in (1, 2, 3) for c in (0, 1)]
    for partner in partners:
        pl.semaphore_signal(barrier, inc=1, device_id=partner, device_id_type=MESH)

    pending = []

    def copy(src, dst, send, recv, to):
        return pltpu.make_async_remote_copy(
            src_ref=src, dst_ref=dst, send_sem=send, recv_sem=recv, device_id=to, device_id_type=MESH
        )

    def send(src, dst, ssem, rsem, to):
        one = copy(src, dst, ssem, rsem, to)
        one.start()
        pending.append((None, one))

    def send_when(cond, *copies):
        made = [copy(*c) for c in copies]

        @pl.when(cond)
        def _():
            for one in made:
                one.start()

        pending.extend((cond, one) for one in made)

    def landed(dst, rsem):
        copy(dst, dst, e_s.at[0], rsem, sibling).wait_recv()

    sharp, off = sharp_ref[0], off_ref[0]

    fetch_text.wait()
    jbuf[0:HALF, :] = unit_rows(cap[...])[1].astype(BF16)
    fetch_image.wait()

    @pl.when(first)
    def _():
        ibuf[0:ROWS, :] = unit_rows(pic[...])[1].astype(BF16)

    pl.semaphore_wait(barrier, len(partners))

    def irows(slot, half):
        return ibuf.at[pl.ds(slot * ROWS + half * HALF, HALF)]

    def jrows(slot, c, start=0, count=QUARTER):
        return jbuf.at[pl.ds(pl.multiple_of(slot * HALF + c * QUARTER + start, EIGHTH), count)]

    send(jrows(0, core), jrows(2, core), t_s.at[0, 0], t_r.at[0, 0], z_up)
    send(jrows(0, core), jrows(1, core), t_s.at[1, 0], t_r.at[1, 0], z_down)

    def to_y(slot, half):
        target = y_down1 if half else y_up1
        return (irows(slot, half), irows(slot, half), i_s.at[6 + 2 * slot + half], i_r.at[slot, half], target)

    send_when(
        first,
        (irows(0, 0), irows(1, 0), i_s.at[0], i_r.at[1, 0], x_up),
        (irows(0, 1), irows(2, 1), i_s.at[1], i_r.at[2, 1], x_down),
        to_y(0, 0),
        to_y(0, 1),
        (irows(0, 1), irows(1, 1), i_s.at[2], i_r.at[1, 1], x_up),
        (irows(0, 0), irows(2, 0), i_s.at[3], i_r.at[2, 0], x_down),
    )

    lacc[...] = jnp.zeros_like(lacc)

    def swap(slot):
        send(jrows(slot, core), jrows(slot, core), d_s.at[slot], d_r.at[slot], sibling)

    def swapped(*slots):
        for slot in slots:
            landed(jrows(slot, other), d_r.at[slot])

    def text_hop(d):
        if d < 4:
            landed(jrows(2 * d, core), t_r.at[0, d - 1])
            landed(jrows(2 * d - 1, core), t_r.at[1, d - 1])
        else:
            landed(jrows(7, core, 0, EIGHTH), t_r.at[0, 3])
            landed(jrows(7, core, EIGHTH, EIGHTH), t_r.at[1, 3])
        if d < 3:
            send(jrows(2 * d, core), jrows(2 * d + 2, core), t_s.at[0, d], t_r.at[0, d], z_up)
            send(jrows(2 * d - 1, core), jrows(2 * d + 1, core), t_s.at[1, d], t_r.at[1, d], z_down)
        elif d == 3:
            send(jrows(6, core, 0, EIGHTH), jrows(7, core, 0, EIGHTH), t_s.at[0, 3], t_r.at[0, 3], z_up)
            send(
                jrows(5, core, EIGHTH, EIGHTH), jrows(7, core, EIGHTH, EIGHTH), t_s.at[1, 3], t_r.at[1, 3], z_down
            )
        if d < 4:
            swap(2 * d - 1)
            swap(2 * d)
        else:
            swap(7)

    log2_e = 1.4426950408889634
    sharp2, off2 = sharp * log2_e, off * log2_e

    def logits_block(i, j):
        ri, rj = slice(i * ROWS, (i + 1) * ROWS), slice(j * ROWS, (j + 1) * ROWS)
        logits = sharp2 * contract(ibuf[ri, :], jbuf[rj, :], ((1,), (1,))) + off2
        if (i, j) == (0, 0):
            row = lax.broadcasted_iota(jnp.int32, (ROWS, ROWS), 0)
            col = lax.broadcasted_iota(jnp.int32, (ROWS, ROWS), 1)
            same = jnp.logical_and(jnp.logical_and(row == col + yh * HALF, col < HALF), first)
            logits = jnp.where(same, -logits, logits)
        grown = jnp.exp2(logits)
        total = 1.0 + grown
        rough = pl.reciprocal(total, approx=True)
        inverse = rough * (2.0 - total * rough)
        coef = grown * inverse
        lost = (grown - (total - 1.0)) * inverse
        lacc[ri, :] += jnp.log(total[:, :HALF] * total[:, HALF:]) + (lost[:, :HALF] + lost[:, HALF:])
        if (i, j) == (0, 0):
            coef = jnp.where(same, -coef, coef)
        coef = coef.astype(BF16)
        cbuf[ri, rj] = coef
        ctbuf[rj, ri] = coef.T

    def product(out, left, right, m, k0, k1):
        rows, depth = slice(m * ROWS, (m + 1) * ROWS), slice(k0 * ROWS, k1 * ROWS)
        a = left[rows, depth]
        for n in range(0, WIDTH, 256):
            columns = slice(n, min(n + 256, WIDTH))
            result = contract(a, right[depth, columns], ((1,), (0,)))
            out[rows, columns] = result if k0 == 0 else out[rows, columns] + result

    def image_product(i, j0, j1):
        product(pacc, cbuf, jbuf, i, j0, j1)

    def text_product(j, i0, i1):
        product(tacc, ctbuf, ibuf, j, i0, i1)

    @pl.when(first)
    def _():
        landed(irows(1, 0), i_r.at[1, 0])
        landed(irows(2, 1), i_r.at[2, 1])

    send_when(
        first,
        (irows(1, 0), irows(3, 0), i_s.at[4], i_r.at[3, 0], x_up),
        (irows(2, 1), irows(3, 1), i_s.at[5], i_r.at[3, 1], x_down),
        to_y(1, 0),
        to_y(2, 1),
    )
    text_hop(1)

    @pl.when(second)
    def _():
        landed(irows(0, 0), i_r.at[0, 0])
        landed(irows(0, 1), i_r.at[0, 1])

    swapped(1)
    logits_block(0, 0)

    @pl.when(first)
    def _():
        landed(irows(1, 1), i_r.at[1, 1])
        landed(irows(2, 0), i_r.at[2, 0])

    send_when(first, to_y(1, 1), to_y(2, 0))
    text_hop(2)
    swapped(2, 3)
    logits_block(0, 1)

    @pl.when(first)
    def _():
        landed(irows(3, 0), i_r.at[3, 0])
        landed(irows(3, 1), i_r.at[3, 1])

    send_when(first, to_y(3, 0), to_y(3, 1))
    text_hop(3)

    @pl.when(second)
    def _():
        for slot in (1, 2):
            for half in (0, 1):
                landed(irows(slot, half), i_r.at[slot, half])

    logits_block(1, 0)
    image_product(0, 0, 2)
    logits_block(2, 0)
    logits_block(1, 1)
    text_product(0, 0, 3)
    logits_block(2, 1)
    swapped(4, 5)
    logits_block(0, 2)
    text_product(1, 0, 3)
    logits_block(1, 2)
    image_product(1, 0, 2)
    logits_block(2, 2)
    text_hop(4)
    image_product(2, 0, 3)
    text_product(2, 0, 3)
    swapped(6, 7)
    logits_block(0, 3)
    logits_block(1, 3)
    image_product(1, 2, 4)
    logits_block(2, 3)
    image_product(2, 3, 4)
    text_product(3, 0, 3)

    @pl.when(second)
    def _():
        landed(irows(3, 0), i_r.at[3, 0])
        landed(irows(3, 1), i_r.at[3, 1])

    logits_block(3, 0)
    logits_block(3, 1)
    logits_block(3, 2)
    logits_block(3, 3)
    image_product(3, 0, 4)

    up_hi = lax.rem(y + 1, NY) // 2
    turns = (
        other * 2 * (1 - yh) + core * (2 * up_hi + 1),
        other * (2 * yh + 1) + core * 2 * up_hi,
        other * (2 * (1 - yh) + 1) + core * 2 * (1 - up_hi),
        other * 2 * yh + core * (2 * (1 - up_hi) + 1),
    )

    def seat(k):
        return pl.ds(k * QUARTER, QUARTER)

    def part_rows(slot, k):
        return pl.ds(pl.multiple_of(slot * ROWS + turns[k] * QUARTER, QUARTER), QUARTER)

    def far_turn(k):
        pb[0, seat(k), :] = pacc[part_rows(3, k), :].astype(BF16)
        send(pb.at[0, seat(k)], xr1.at[seat(k)], x1_s.at[k], x1_r.at[k], x_up if k < 2 else x_down)

    def near_turn(slot, k):
        side = 0 if slot == 2 else 1
        rows = pacc[part_rows(slot, k), :]
        if (k < 2) == (slot == 2):
            landed(xr1.at[seat(k)], x1_r.at[k])
            rows = rows + xr1[seat(k), :].astype(F32)
        pb[1 + side, seat(k), :] = rows.astype(BF16)
        send(
            pb.at[1 + side, seat(k)],
            x2.at[side, seat(k)],
            x2_s.at[side, k],
            x2_r.at[side, k],
            x_down if side else x_up,
        )

    def text_over(*slots):
        for slot in slots:
            mine = pl.ds(pl.multiple_of(slot * HALF + other * QUARTER, QUARTER), QUARTER)
            ts[slot] = tacc[mine, :].astype(BF16)
            send(ts.at[slot], tr.at[slot], e_s.at[slot], e_r.at[slot], sibling)

    for k in (0, 2, 1, 3):
        far_turn(k)
    text_product(3, 3, 4)
    text_over(7, 6)
    near_turn(2, 2)
    near_turn(1, 0)
    near_turn(2, 3)
    near_turn(1, 1)
    text_product(2, 3, 4)
    text_over(5, 4)
    text_product(1, 3, 4)
    text_product(0, 3, 4)
    text_over(3, 2, 1, 0)
    image_product(0, 2, 4)

    ones = jnp.ones((8, HALF), F32)
    for i in range(4):
        ls[i] = lax.dot_general(
            ones,
            lacc[i * ROWS : (i + 1) * ROWS, :],
            (((1,), (1,)), ((), ())),
            precision=lax.Precision.HIGHEST,
            preferred_element_type=F32,
        )
    send(ls.at[2], lx.at[0], lx_s.at[0], lx_r.at[0], x_up)
    send(ls.at[1], lx.at[1], lx_s.at[1], lx_r.at[1], x_down)
    send(ls.at[3], lx.at[2], lx_s.at[2], lx_r.at[2], x_far)

    def text_sum(slot):
        landed(tr.at[slot], e_r.at[slot])
        mine = pl.ds(pl.multiple_of(slot * HALF + core * QUARTER, QUARTER), QUARTER)
        return tacc[mine, :] + tr[slot].astype(F32)

    def text_back(d):
        if d == 4:
            both = text_sum(7).astype(BF16)
            for side in (0, 1):
                vs[side, 3, 0:EIGHTH, :] = both[side * EIGHTH : (side + 1) * EIGHTH]
                part = pl.ds(0, EIGHTH)
                send(
                    vs.at[side, 3, part],
                    vr.at[side, 3, part],
                    v_s.at[side, 3],
                    v_r.at[side, 3],
                    z_down if side else z_up,
                )
            return
        for side in (0, 1):
            rows = text_sum(2 * d if side else 2 * d - 1)
            if d == 3:
                part = pl.ds(0, EIGHTH)
                landed(vr.at[side, 3, part], v_r.at[side, 3])
                came = vr[side, 3, 0:EIGHTH, :].astype(F32)
                if side:
                    vs[side, 2, 0:EIGHTH, :] = rows[:EIGHTH].astype(BF16)
                    vs[side, 2, EIGHTH:QUARTER, :] = (rows[EIGHTH:] + came).astype(BF16)
                else:
                    vs[side, 2, 0:EIGHTH, :] = (rows[:EIGHTH] + came).astype(BF16)
                    vs[side, 2, EIGHTH:QUARTER, :] = rows[EIGHTH:].astype(BF16)
            else:
                landed(vr.at[side, d], v_r.at[side, d])
                vs[side, d - 1] = (rows + vr[side, d].astype(F32)).astype(BF16)
            send(
                vs.at[side, d - 1],
                vr.at[side, d - 1],
                v_s.at[side, d - 1],
                v_r.at[side, d - 1],
                z_down if side else z_up,
            )

    text_back(4)
    near_turn(2, 0)
    near_turn(1, 2)
    text_back(3)
    near_turn(2, 1)
    near_turn(1, 3)
    text_back(2)

    source = yh + 2 * core
    block_yl = lax.rem(yl + core, 2)

    def owner_of(q):
        to = at(x, 2 * (q // 2) + block_yl, z, q % 2)
        return to, jnp.logical_and(dp == to[0], split == to[1])

    for k in range(3):
        landed(lx.at[k], lx_r.at[k])
    rl[...] = ls[0] + lx[0] + lx[1] + lx[2]
    for q in range(4):
        to, own = owner_of(q)
        send_when(jnp.logical_not(own), (rl, lq.at[source], ly_s.at[q], ly_r.at[source], to))

        @pl.when(own)
        def _():
            lq[source] = rl[...]

    text_back(1)

    y_up0, y_down0 = at(x, y + 1, z, 0), at(x, y + 3, z, 0)

    def image_sum(k):
        landed(x2.at[0, seat(k)], x2_r.at[0, k])
        landed(x2.at[1, seat(k)], x2_r.at[1, k])
        return pacc[part_rows(0, k), :] + (x2[0, seat(k), :].astype(F32) + x2[1, seat(k), :].astype(F32))

    def image_out(k):
        total = image_sum(k)
        rb[seat(k), :] = total.astype(BF16)
        if k == 0:
            box = other * 3 + core
            send(rb.at[seat(0)], qr.at[box], y_s.at[0], y_r.at[box], y_up1)
        elif k == 2:
            box = other * 4 + core * 2
            send(rb.at[seat(2)], qr.at[box], y_s.at[2], y_r.at[box], (y_down1[0], y_down0[1] + other))
        else:
            carried = 3 if k == 1 else 4
            box, to = (1, y_up0) if k == 1 else (2, y_down1)

            @pl.when(second)
            def _():
                landed(qr.at[carried], y_r.at[carried])
                rb[seat(k), :] = (total + qr[carried].astype(F32)).astype(BF16)

            send_when(second, (rb.at[seat(k)], qr.at[box], y_s.at[k], y_r.at[box], to))
            if k == 1:
                send_when(first, (rb.at[seat(1)], qr.at[0], y_s.at[1], y_r.at[0], sibling))
            else:

                @pl.when(first)
                def _():
                    qr[0] = rb[seat(3), :]

    image_out(0)
    image_out(2)

    mine = yh * 2 + core
    outs = (img_out, txt_out)

    def quarter_rows(q, start=0, count=QUARTER):
        return pl.ds(pl.multiple_of(q * QUARTER + start, EIGHTH), count)

    my_rows = quarter_rows(mine)
    y_up, y_down = at(x, y + 1, z, core), at(x, y + 3, z, core)

    def gather_out(kind, grad, values):
        inverse, unit = unit_rows(values)
        out = outs[kind]
        out[my_rows, :] = unit_back(unit, inverse, sharp * grad).astype(BF16)
        low, high = out.at[quarter_rows(mine, 0, EIGHTH)], out.at[quarter_rows(mine, EIGHTH, EIGHTH)]
        send(low, hop.at[kind, 0], g_s.at[kind, 0], g_r.at[kind, 0], y_up)
        send(high, hop.at[kind, 1], g_s.at[kind, 1], g_r.at[kind, 1], y_down)
        send(out.at[my_rows], out.at[my_rows], g_s.at[kind, 2], g_r.at[kind, 2], sibling)

    def gather_on(kind):
        out = outs[kind]
        landed(hop.at[kind, 0], g_r.at[kind, 0])
        there = out.at[quarter_rows(2 * (1 - up_hi) + core, 0, EIGHTH)]
        send(hop.at[kind, 0], there, g_s.at[kind, 3], g_r.at[kind, 3], y_up)
        landed(hop.at[kind, 1], g_r.at[kind, 1])
        there = out.at[quarter_rows(2 * up_hi + core, EIGHTH, EIGHTH)]
        send(hop.at[kind, 1], there, g_s.at[kind, 4], g_r.at[kind, 4], y_down)

    def gather_over(kind):
        for half in (0, 1):
            here = outs[kind].at[quarter_rows((1 - yh) * 2 + core, half * EIGHTH, EIGHTH)]
            landed(here, g_r.at[kind, 3 + half])
            send(here, here, g_s.at[kind, 5 + half], g_r.at[kind, 5 + half], sibling)

    def gather_end(kind):
        landed(outs[kind].at[quarter_rows(yh * 2 + other)], g_r.at[kind, 2])
        for half in (0, 1):
            here = outs[kind].at[quarter_rows((1 - yh) * 2 + other, half * EIGHTH, EIGHTH)]
            landed(here, g_r.at[kind, 5 + half])

    grad = text_sum(0)
    for side in (0, 1):
        landed(vr.at[side, 0], v_r.at[side, 0])
        grad = grad + vr[side, 0].astype(F32)
    gather_out(1, grad, cap[pl.ds(pl.multiple_of(core * QUARTER, QUARTER), QUARTER), :])

    gather_on(1)
    image_out(1)
    image_out(3)
    gather_over(1)

    for k in range(4):
        here = jnp.logical_and(first, yh == k)

        @pl.when(jnp.logical_not(here))
        def _():
            landed(lq.at[k], ly_r.at[k])

    loss_out[...] = ((lq[0] + lq[1]) + (lq[2] + lq[3])) * (1.0 / PAIRS)

    @pl.when(second)
    def _():
        landed(qr.at[0], y_r.at[0])

    landed(qr.at[1], y_r.at[1])
    landed(qr.at[2], y_r.at[2])
    grad = qr[0].astype(F32) + (qr[1].astype(F32) + qr[2].astype(F32))
    gather_out(0, grad, pic[my_rows, :])
    gather_on(0)
    gather_over(0)
    gather_end(1)
    gather_end(0)

    for cond, one in pending:
        if cond is None:
            one.wait_send()
        else:

            @pl.when(cond)
            def _():
                one.wait_send()


def per_device(picture_vectors, caption_vectors, sharpness_entry, offset_shift):
    dma = pltpu.SemaphoreType.DMA
    vmem = pl.BlockSpec(memory_space=pltpu.VMEM)
    smem = pl.BlockSpec(memory_space=pltpu.SMEM)
    hbm = pl.BlockSpec(memory_space=pltpu.HBM)
    img, txt, loss = pl.pallas_call(
        kernel,
        out_shape=(
            jax.ShapeDtypeStruct((ROWS, WIDTH), BF16),
            jax.ShapeDtypeStruct((ROWS, WIDTH), BF16),
            jax.ShapeDtypeStruct((8, ROWS), F32),
        ),
        in_specs=[hbm, hbm, smem, smem],
        out_specs=(vmem, vmem, vmem),
        scratch_shapes=[
            pltpu.VMEM((ROWS, WIDTH), BF16),
            pltpu.VMEM((HALF, WIDTH), BF16),
            pltpu.VMEM((4 * ROWS, WIDTH), BF16),
            pltpu.VMEM((8 * HALF, WIDTH), BF16),
            pltpu.VMEM((4 * ROWS, 8 * HALF), BF16),
            pltpu.VMEM((8 * HALF, 4 * ROWS), BF16),
            pltpu.VMEM((4 * ROWS, WIDTH), F32),
            pltpu.VMEM((8 * HALF, WIDTH), F32),
            pltpu.VMEM((4 * ROWS, HALF), F32),
            pltpu.VMEM((3, ROWS, WIDTH), BF16),
            pltpu.VMEM((ROWS, WIDTH), BF16),
            pltpu.VMEM((2, ROWS, WIDTH), BF16),
            pltpu.VMEM((ROWS, WIDTH), BF16),
            pltpu.VMEM((5, QUARTER, WIDTH), BF16),
            pltpu.VMEM((8, QUARTER, WIDTH), BF16),
            pltpu.VMEM((8, QUARTER, WIDTH), BF16),
            pltpu.VMEM((2, 4, QUARTER, WIDTH), BF16),
            pltpu.VMEM((2, 4, QUARTER, WIDTH), BF16),
            pltpu.VMEM((4, 8, ROWS), F32),
            pltpu.VMEM((3, 8, ROWS), F32),
            pltpu.VMEM((8, ROWS), F32),
            pltpu.VMEM((4, 8, ROWS), F32),
            pltpu.VMEM((2, 2, EIGHTH, WIDTH), BF16),
            dma((2,)),
            dma((14,)), dma((4, 2)),
            dma((2, 4)), dma((2, 4)),
            dma((8,)), dma((8,)),
            dma((4,)), dma((4,)),
            dma((2, 4)), dma((2, 4)),
            dma((4,)), dma((5,)),
            dma((4,)), dma((4,)),
            dma((3,)), dma((3,)),
            dma((8,)), dma((8,)),
            dma((2, 4)), dma((2, 4)),
            dma((2, 7)), dma((2, 7)),
        ],
        compiler_params=pltpu.CompilerParams(
            collective_id=0, has_side_effects=True, vmem_limit_bytes=48 * 1024 * 1024
        ),
        cost_estimate=pl.CostEstimate(flops=7_300_000_000, bytes_accessed=4_000_000, transcendentals=3_000_000),
    )(
        pltpu.with_memory_space_constraint(picture_vectors, pltpu.HBM),
        pltpu.with_memory_space_constraint(caption_vectors, pltpu.HBM),
        sharpness_entry,
        offset_shift,
    )
    return img.astype(F32), txt.astype(F32), loss[0]


def solution(mesh):
    placed = (P("dp", None), P("dp", None), P(), P())
    return jax.shard_map(
        per_device,
        mesh=mesh,
        in_specs=placed,
        out_specs=(P("dp", None), P("dp", None), P("dp")),
        check_vma=False,
    )
```

time: 894 us -> 79.8 us (0.09)
  waiting for transfers between devices: 695 us -> 0 us
  matrix products: 97 us -> 0 us
  Pallas kernels: 0 us -> 74.5 us
  blocking collectives: 48.5 us -> 0 us
  local copies, waits for them, and re-layouts: 17.2 us -> 0.56 us
  between operations: 14.9 us -> 1.93 us
  other arithmetic: 11.9 us -> 2.18 us
    ppermute x38 -> x0, waiting for transfers between devices: 637 us -> none  [passed_along(): return lax.ppermute(value, axis, pairs)]
    dot_general x48 -> x0, matrix products: 97 us -> none  [the longest x16 46.1 us: tile(): lax.dot_general(img_b, block, (((1,), (1,)), ((), ())), preferred_element...]
    pallas_call x0 -> x1, Pallas kernels: none -> 74.5 us  [per_device(): pl.pallas_call(kernel, out_shape=(jax.ShapeDtypeStruct((ROWS, WIDTH), BF1...]
    psum x1 -> x0, waiting for transfers between devices: 58 us -> none  [per_device(): lax.psum((img_acc, text_accumulator, loss_acc), 'split')]
    psum x1 -> x0, blocking collectives: 48.5 us -> none  [per_device(): lax.psum((img_acc, text_accumulator, loss_acc), 'split')]
    while x16 -> x0, local copies, waits for them, and re-layouts: 17.1 us -> none
  transfers between devices with their start and end apart: 39 -> 0, of which waited for: 23 -> 0; matrix products, arithmetic and copies ran while one was open for 2% -> 0% of each run, Pallas kernels for 0% -> 0%
where the time goes in v1:
time: 79.8 us; the launch traced here: 79.2 us
  Pallas kernels  74.5 us (93%)
  other arithmetic  2.18 us (3%)
  between operations  1.93 us (2%)
    pallas_call x1, Pallas kernels, per_device(): pl.pallas_call(kernel, out_shape=(jax.ShapeDtypeStruct((ROWS, WIDTH), BF1...  74.5 us
    convert_element_type x2, other arithmetic, per_device(): return (img.astype(F32), txt.astype(F32), loss[0])  2.18 us

profile of v1, /device:TPU:1, one launch (start us, length us, event | category | flops | bytes accessed | tf_op | source)
XLA Modules:
  0.0 79.2 jit_solution(6882052504289506782)
XLA Ops:
  1.9 74.5 %shard_map.67 = (bf16[256,1152]{1,0:T(8,128)(2,1)S(1)}, bf16[256,1152]{1,0:T(8,128)(2,1)S(1)}, f32[8,256]{1,0:T(8,128)S(1)}) custom-call(bf16[256,1152]{1,0:T(8,128)(2,1)} %pic_hbm.1, bf16[256,1152]{1,0:T(8,128)(2,1)} %cap_hbm.1, f32[1]{0:T(128)S(6)} %copy.7.sharp_ref, f32[1]{0:T(128)S(6)} %copy.8.off_ref), custom_call_target="tpu_custom_call" | custom-call | flops 7299999744 | bytes 4000000 | tf_op jit(solution)/shard_map/pallas_call | solution.py:543
  76.5 0.6 slice.3
  77.0 1.1 %convert_element_type.6 = f32[256,1152]{1,0:T(8,128)} convert(bf16[256,1152]{1,0:T(8,128)(2,1)S(1)} %get-tuple-element.6) | non-fusion elementwise | flops 294912 | bytes 1769472 | tf_op jit(solution)/shard_map/convert_element_type | solution.py:599
  78.1 1.1 %convert_element_type.7 = f32[256,1152]{1,0:T(8,128)} convert(bf16[256,1152]{1,0:T(8,128)(2,1)S(1)} %get-tuple-element.7) | non-fusion elementwise | flops 294912 | bytes 1769472 | tf_op jit(solution)/shard_map/convert_element_type | solution.py:599

commit v2 on v1

--- a/solution.py
+++ b/solution.py
@@ -1,3 +1,5 @@
+import math
+
 import jax
 import jax.numpy as jnp
 from jax import lax
@@ -93,10 +95,24 @@
 
         pending.extend((cond, one) for one in made)
 
+    def drain():
+        for cond in (None, first, second):
+            some = [one for c, one in pending if c is cond]
+            if cond is None:
+                for one in some:
+                    one.wait_send()
+            elif some:
+
+                @pl.when(cond)
+                def _():
+                    for one in some:
+                        one.wait_send()
+
+        pending[:] = [(c, one) for c, one in pending if not any(c is k for k in (None, first, second))]
+
     def landed(dst, rsem):
         copy(dst, dst, e_s.at[0], rsem, sibling).wait_recv()
 
-    sharp, off = sharp_ref[0], off_ref[0]
 
     fetch_text.wait()
     jbuf[0:HALF, :] = unit_rows(cap[...])[1].astype(BF16)
@@ -161,15 +177,17 @@
         else:
             swap(7)
 
+    sharp, off = sharp_ref[0], off_ref[0]
     log2_e = 1.4426950408889634
     sharp2, off2 = sharp * log2_e, off * log2_e
 
-    def logits_block(i, j):
-        ri, rj = slice(i * ROWS, (i + 1) * ROWS), slice(j * ROWS, (j + 1) * ROWS)
+    def logits_block(i0, i1, j0, j1):
+        ri, rj = slice(i0 * ROWS, i1 * ROWS), slice(j0 * ROWS, j1 * ROWS)
         logits = sharp2 * contract(ibuf[ri, :], jbuf[rj, :], ((1,), (1,))) + off2
-        if (i, j) == (0, 0):
-            row = lax.broadcasted_iota(jnp.int32, (ROWS, ROWS), 0)
-            col = lax.broadcasted_iota(jnp.int32, (ROWS, ROWS), 1)
+        diagonal = i0 == 0 and j0 == 0
+        if diagonal:
+            row = lax.broadcasted_iota(jnp.int32, logits.shape, 0)
+            col = lax.broadcasted_iota(jnp.int32, logits.shape, 1)
             same = jnp.logical_and(jnp.logical_and(row == col + yh * HALF, col < HALF), first)
             logits = jnp.where(same, -logits, logits)
         grown = jnp.exp2(logits)
@@ -178,26 +196,28 @@
         inverse = rough * (2.0 - total * rough)
         coef = grown * inverse
         lost = (grown - (total - 1.0)) * inverse
-        lacc[ri, :] += jnp.log(total[:, :HALF] * total[:, HALF:]) + (lost[:, :HALF] + lost[:, HALF:])
-        if (i, j) == (0, 0):
+        strips = [slice(n, n + HALF) for n in range(0, (j1 - j0) * ROWS, HALF)]
+        loss = lacc[ri, :]
+        for n in range(0, len(strips), 4):
+            group = strips[n : n + 4]
+            loss = loss + (jnp.log(math.prod(total[:, c] for c in group)) + sum(lost[:, c] for c in group))
+        lacc[ri, :] = loss
+        if diagonal:
             coef = jnp.where(same, -coef, coef)
         coef = coef.astype(BF16)
         cbuf[ri, rj] = coef
         ctbuf[rj, ri] = coef.T
 
-    def product(out, left, right, m, k0, k1):
-        rows, depth = slice(m * ROWS, (m + 1) * ROWS), slice(k0 * ROWS, k1 * ROWS)
-        a = left[rows, depth]
-        for n in range(0, WIDTH, 256):
-            columns = slice(n, min(n + 256, WIDTH))
-            result = contract(a, right[depth, columns], ((1,), (0,)))
-            out[rows, columns] = result if k0 == 0 else out[rows, columns] + result
-
-    def image_product(i, j0, j1):
-        product(pacc, cbuf, jbuf, i, j0, j1)
-
-    def text_product(j, i0, i1):
-        product(tacc, ctbuf, ibuf, j, i0, i1)
+    def product(out, left, right, m0, m1, k0, k1):
+        rows, depth = slice(m0 * ROWS, m1 * ROWS), slice(k0 * ROWS, k1 * ROWS)
+        result = contract(left[rows, depth], right[depth, :], ((1,), (0,)))
+        out[rows, :] = result if k0 == 0 else out[rows, :] + result
+
+    def image_product(i0, i1, j0, j1):
+        product(pacc, cbuf, jbuf, i0, i1, j0, j1)
+
+    def text_product(j0, j1, i0, i1):
+        product(tacc, ctbuf, ibuf, j0, j1, i0, i1)
 
     @pl.when(first)
     def _():
@@ -219,7 +239,7 @@
         landed(irows(0, 1), i_r.at[0, 1])
 
     swapped(1)
-    logits_block(0, 0)
+    logits_block(0, 1, 0, 1)
 
     @pl.when(first)
     def _():
@@ -229,7 +249,7 @@
     send_when(first, to_y(1, 1), to_y(2, 0))
     text_hop(2)
     swapped(2, 3)
-    logits_block(0, 1)
+    logits_block(0, 1, 1, 2)
 
     @pl.when(first)
     def _():
@@ -245,39 +265,24 @@
             for half in (0, 1):
                 landed(irows(slot, half), i_r.at[slot, half])
 
-    logits_block(1, 0)
-    image_product(0, 0, 2)
-    logits_block(2, 0)
-    logits_block(1, 1)
-    text_product(0, 0, 3)
-    logits_block(2, 1)
+    logits_block(1, 3, 0, 2)
     swapped(4, 5)
-    logits_block(0, 2)
-    text_product(1, 0, 3)
-    logits_block(1, 2)
-    image_product(1, 0, 2)
-    logits_block(2, 2)
+    logits_block(0, 3, 2, 3)
+    image_product(0, 3, 0, 3)
     text_hop(4)
-    image_product(2, 0, 3)
-    text_product(2, 0, 3)
+    text_product(0, 3, 0, 3)
     swapped(6, 7)
-    logits_block(0, 3)
-    logits_block(1, 3)
-    image_product(1, 2, 4)
-    logits_block(2, 3)
-    image_product(2, 3, 4)
-    text_product(3, 0, 3)
+    logits_block(0, 3, 3, 4)
+    image_product(1, 3, 3, 4)
+    text_product(3, 4, 0, 3)
 
     @pl.when(second)
     def _():
         landed(irows(3, 0), i_r.at[3, 0])
         landed(irows(3, 1), i_r.at[3, 1])
 
-    logits_block(3, 0)
-    logits_block(3, 1)
-    logits_block(3, 2)
-    logits_block(3, 3)
-    image_product(3, 0, 4)
+    logits_block(3, 4, 0, 4)
+    image_product(3, 4, 0, 4)
 
     up_hi = lax.rem(y + 1, NY) // 2
     turns = (
@@ -312,26 +317,29 @@
             x_down if side else x_up,
         )
 
-    def text_over(*slots):
-        for slot in slots:
+    def text_over(low, count):
+        for slot in range(low, low + count):
             mine = pl.ds(pl.multiple_of(slot * HALF + other * QUARTER, QUARTER), QUARTER)
             ts[slot] = tacc[mine, :].astype(BF16)
-            send(ts.at[slot], tr.at[slot], e_s.at[slot], e_r.at[slot], sibling)
+        slots = pl.ds(low, count)
+        send(ts.at[slots], tr.at[slots], e_s.at[low], e_r.at[low], sibling)
+
+    def text_came(low, count):
+        landed(tr.at[pl.ds(low, count)], e_r.at[low])
 
     for k in (0, 2, 1, 3):
         far_turn(k)
-    text_product(3, 3, 4)
-    text_over(7, 6)
+    text_product(3, 4, 3, 4)
+    text_over(6, 2)
     near_turn(2, 2)
     near_turn(1, 0)
     near_turn(2, 3)
     near_turn(1, 1)
-    text_product(2, 3, 4)
-    text_over(5, 4)
-    text_product(1, 3, 4)
-    text_product(0, 3, 4)
-    text_over(3, 2, 1, 0)
-    image_product(0, 2, 4)
+    text_product(2, 3, 3, 4)
+    text_over(4, 2)
+    text_product(0, 2, 3, 4)
+    text_over(0, 4)
+    image_product(0, 1, 3, 4)
 
     ones = jnp.ones((8, HALF), F32)
     for i in range(4):
@@ -347,7 +355,6 @@
     send(ls.at[3], lx.at[2], lx_s.at[2], lx_r.at[2], x_far)
 
     def text_sum(slot):
-        landed(tr.at[slot], e_r.at[slot])
         mine = pl.ds(pl.multiple_of(slot * HALF + core * QUARTER, QUARTER), QUARTER)
         return tacc[mine, :] + tr[slot].astype(F32)
 
@@ -388,12 +395,15 @@
                 z_down if side else z_up,
             )
 
+    text_came(6, 2)
     text_back(4)
     near_turn(2, 0)
     near_turn(1, 2)
+    text_came(4, 2)
     text_back(3)
     near_turn(2, 1)
     near_turn(1, 3)
+    text_came(0, 4)
     text_back(2)
 
     source = yh + 2 * core
@@ -415,6 +425,7 @@
             lq[source] = rl[...]
 
     text_back(1)
+    drain()
 
     y_up0, y_down0 = at(x, y + 1, z, 0), at(x, y + 3, z, 0)
 
@@ -498,10 +509,9 @@
         grad = grad + vr[side, 0].astype(F32)
     gather_out(1, grad, cap[pl.ds(pl.multiple_of(core * QUARTER, QUARTER), QUARTER), :])
 
-    gather_on(1)
     image_out(1)
     image_out(3)
-    gather_over(1)
+    gather_on(1)
 
     for k in range(4):
         here = jnp.logical_and(first, yh == k)
@@ -520,6 +530,8 @@
     landed(qr.at[2], y_r.at[2])
     grad = qr[0].astype(F32) + (qr[1].astype(F32) + qr[2].astype(F32))
     gather_out(0, grad, pic[my_rows, :])
+    gather_over(1)
+    drain()
     gather_on(0)
     gather_over(0)
     gather_end(1)

time: 79.8 us -> 80.7 us (1.011)
  Pallas kernels: 74.5 us -> 75.9 us
    pallas_call x1, Pallas kernels: 74.5 us -> 75.9 us  [per_device(): pl.pallas_call(kernel, out_shape=(jax.ShapeDtypeStruct((ROWS, WIDTH), BF1...]
where the time goes in v2:
time: 80.7 us; the launch traced here: 80.6 us
  Pallas kernels  75.9 us (94%)
  other arithmetic  2.18 us (3%)
  between operations  1.93 us (2%)
    pallas_call x1, Pallas kernels, per_device(): pl.pallas_call(kernel, out_shape=(jax.ShapeDtypeStruct((ROWS, WIDTH), BF1...  75.9 us
    convert_element_type x2, other arithmetic, per_device(): return (img.astype(F32), txt.astype(F32), loss[0])  2.18 us

profile of v2, /device:TPU:1, one launch (start us, length us, event | category | flops | bytes accessed | tf_op | source)
XLA Modules:
  0.0 80.6 jit_solution(12351717533219865754)
XLA Ops:
  1.9 75.9 %shard_map.67 = (bf16[256,1152]{1,0:T(8,128)(2,1)S(1)}, bf16[256,1152]{1,0:T(8,128)(2,1)S(1)}, f32[8,256]{1,0:T(8,128)S(1)}) custom-call(bf16[256,1152]{1,0:T(8,128)(2,1)} %pic_hbm.1, bf16[256,1152]{1,0:T(8,128)(2,1)} %cap_hbm.1, f32[1]{0:T(128)S(6)} %copy.7.sharp_ref, f32[1]{0:T(128)S(6)} %copy.8.off_ref), custom_call_target="tpu_custom_call" | custom-call | flops 7299999744 | bytes 4000000 | tf_op jit(solution)/shard_map/pallas_call | solution.py:555
  77.8 0.6 slice.3
  78.4 1.1 %convert_element_type.6 = f32[256,1152]{1,0:T(8,128)} convert(bf16[256,1152]{1,0:T(8,128)(2,1)S(1)} %get-tuple-element.6) | non-fusion elementwise | flops 294912 | bytes 1769472 | tf_op jit(solution)/shard_map/convert_element_type | solution.py:611
  79.5 1.1 %convert_element_type.7 = f32[256,1152]{1,0:T(8,128)} convert(bf16[256,1152]{1,0:T(8,128)(2,1)S(1)} %get-tuple-element.7) | non-fusion elementwise | flops 294912 | bytes 1769472 | tf_op jit(solution)/shard_map/convert_element_type | solution.py:611

commit v3 on v1

v3 whole, which is shorter than its diff:
```python
import jax
import jax.numpy as jnp
from jax import lax
from jax.experimental import pallas as pl
from jax.experimental.pallas import tpu as pltpu
from jax.sharding import PartitionSpec as P

MESH = pl.DeviceIdType.MESH
F32 = jnp.float32
BF16 = jnp.bfloat16

NX, NY, NZ = 4, 4, 8
ROWS, WIDTH = 256, 1152
HALF, QUARTER, EIGHTH = 128, 64, 32
PAIRS = 16384


def unit_rows(values):
    values = values.astype(F32)
    inverse = lax.rsqrt(jnp.sum(values * values, axis=1, keepdims=True) + 1e-06)
    return inverse, values * inverse


def unit_back(unit, inverse, grad):
    return (grad - unit * jnp.sum(unit * grad, axis=1, keepdims=True)) * inverse


def contract(a, b, dims):
    return lax.dot_general(a, b, (dims, ((), ())), preferred_element_type=F32)


def kernel(
    pic_hbm, cap_hbm, sharp_ref, off_ref,
    both_out, loss_out,
    pic, cap, ibuf, jbuf, cbuf, ctbuf, pacc, tacc, lacc,
    pb, xr1, x2, rb, qr, ys, yr,
    ts, tr, vs, vr,
    ls, lx, rl, lq,
    hop,
    in_sem, i_s, i_r, t_s, t_r, d_s, d_r, x1_s, x1_r, x2_s, x2_r, y_s, y_r, yc_s, yc_r,
    ly_s, ly_r, lx_s, lx_r, e_s, e_r, v_s, v_r, g_s, g_r,
):
    dp, split = lax.axis_index("dp"), lax.axis_index("split")
    x = lax.rem(dp, NX)
    yl = lax.rem(dp // NX, 2)
    z = dp // (2 * NX)
    yh, core = split // 2, lax.rem(split, 2)
    y = 2 * yh + yl
    other = 1 - core
    first = core == 0
    second = core == 1

    def at(px, py, pz, pc):
        px, py, pz = lax.rem(px, NX), lax.rem(py, NY), lax.rem(pz, NZ)
        return ((pz * 2 + lax.rem(py, 2)) * NX + px, (py // 2) * 2 + pc)

    sibling = at(x, y, z, other)
    x_up, x_down, x_far = (at(x + k, y, z, core) for k in (1, 3, 2))
    z_up, z_down = at(x, y, z + 1, core), at(x, y, z + 7, core)
    y_up1, y_down1 = at(x, y + 1, z, 1), at(x, y + 3, z, 1)

    own_text = pl.multiple_of(yh * HALF, HALF)
    fetch_text = pltpu.make_async_copy(cap_hbm.at[pl.ds(own_text, HALF)], cap, in_sem.at[0])
    fetch_image = pltpu.make_async_copy(pic_hbm, pic, in_sem.at[1])
    fetch_text.start()
    fetch_image.start()

    barrier = pltpu.get_barrier_semaphore()
    partners = [sibling, x_up, x_down, x_far, z_up, z_down]
    partners += [at(x, y + k, z, c) for k in (1, 2, 3) for c in (0, 1)]
    for partner in partners:
        pl.semaphore_signal(barrier, inc=1, device_id=partner, device_id_type=MESH)

    pending = []

    def copy(src, dst, send, recv, to):
        return pltpu.make_async_remote_copy(
            src_ref=src, dst_ref=dst, send_sem=send[0].at[send[1:]], recv_sem=recv, device_id=to, device_id_type=MESH
        )

    def note(cond, src, ssem):
        rows = 0 if src.dtype == F32 else src.shape[0] * (src.shape[1] if len(src.shape) == 3 else 1)
        pending.append((cond, rows, ssem))

    def sent(rows, ssem):
        ref = ibuf.at[pl.ds(0, rows)] if rows else ls.at[0]
        copy(ref, ref, ssem, e_r.at[0], sibling).wait_send()

    branch = [None]

    def on(cond):
        def run(body):
            branch[0] = cond
            pl.when(cond)(body)
            branch[0] = None

        return run

    def send(src, dst, ssem, rsem, to):
        copy(src, dst, ssem, rsem, to).start()
        note(branch[0], src, ssem)

    def send_when(cond, *copies):
        @pl.when(cond)
        def _():
            for one in copies:
                copy(*one).start()

        for one in copies:
            note(cond, one[0], one[2])

    def drain(of=None):
        later = [entry for entry in pending if of is not None and not any(entry[2][0] is sem for sem in of)]
        pending[:] = [entry for entry in pending if not any(entry is k for k in later)]
        for cond in (None, first, second):
            some = [entry[1:] for entry in pending if entry[0] is cond]
            if cond is None:
                for entry in some:
                    sent(*entry)
            elif some:

                @pl.when(cond)
                def _():
                    for entry in some:
                        sent(*entry)

        pending[:] = later + [entry for entry in pending if not any(entry[0] is k for k in (None, first, second))]

    def landed(dst, rsem):
        copy(dst, dst, (e_s, 0), rsem, sibling).wait_recv()


    fetch_text.wait()
    jbuf[0:HALF, :] = unit_rows(cap[...])[1].astype(BF16)
    fetch_image.wait()

    @pl.when(first)
    def _():
        ibuf[0:ROWS, :] = unit_rows(pic[...])[1].astype(BF16)

    pl.semaphore_wait(barrier, len(partners))

    def irows(slot, piece):
        return ibuf.at[pl.ds(slot * ROWS + piece * QUARTER, QUARTER)]

    def jrows(slot, c, start=0, count=QUARTER):
        return jbuf.at[pl.ds(pl.multiple_of(slot * HALF + c * QUARTER + start, EIGHTH), count)]

    def text_piece(slot, piece):
        return jrows(slot, core, piece * EIGHTH, EIGHTH)

    def text_send(side, d, piece, source, target):
        send(
            text_piece(source, piece),
            text_piece(target, piece),
            (t_s, side, d, piece),
            t_r.at[side, d, piece],
            z_down if side else z_up,
        )

    for piece in (0, 1):
        text_send(0, 0, piece, 0, 2)
        text_send(1, 0, piece, 0, 1)

    def to_y(slot, piece):
        target = y_up1 if piece < 2 else y_down1
        return (irows(slot, piece), irows(slot, piece), (i_s, 2 + slot, piece), i_r.at[slot, piece], target)

    def to_x(source, slot, piece, kind):
        target = x_up if slot == 1 or (slot == 3 and piece < 2) else x_down
        return (irows(source, piece), irows(slot, piece), (i_s, kind, piece), i_r.at[slot, piece], target)

    send_when(
        first,
        to_x(0, 1, 0, 0), to_x(0, 2, 2, 1), to_y(0, 0), to_y(0, 2),
        to_x(0, 1, 1, 0), to_x(0, 2, 3, 1), to_y(0, 1), to_y(0, 3),
        to_x(0, 1, 2, 0), to_x(0, 2, 0, 1), to_x(0, 1, 3, 0), to_x(0, 2, 1, 1),
    )

    def pass_near(up, down, onward):
        landed(irows(1, up), i_r.at[1, up])
        if onward:
            send(*to_x(1, 3, up, 6))
        send(*to_y(1, up))
        landed(irows(2, down), i_r.at[2, down])
        if onward:
            send(*to_x(2, 3, down, 6))
        send(*to_y(2, down))

    def pass_far(*pieces):
        for piece in pieces:
            landed(irows(3, piece), i_r.at[3, piece])
            send(*to_y(3, piece))

    def images_in(*slots):
        for slot in slots:
            for piece in range(4):
                landed(irows(slot, piece), i_r.at[slot, piece])

    for zeroed in (lacc,):

        def clear(n, carry):
            rows = pl.ds(pl.multiple_of(n * QUARTER, QUARTER), QUARTER)
            zeroed[rows, :] = jnp.zeros((QUARTER, zeroed.shape[1]), F32)
            return carry

        lax.fori_loop(0, 16, clear, 0)

    def swap(slot):
        send(jrows(slot, core), jrows(slot, core), (d_s, slot), d_r.at[slot], sibling)

    def swapped(*slots):
        for slot in slots:
            landed(jrows(slot, other), d_r.at[slot])

    def text_hop(d, pieces=(0, 1)):
        for piece in pieces:
            for side in (0, 1):
                if d == 4:
                    if piece == side:
                        landed(text_piece(7, piece), t_r.at[side, 3, piece])
                    continue
                here = 2 * d - side
                landed(text_piece(here, piece), t_r.at[side, d - 1, piece])
                if d < 3:
                    text_send(side, d, piece, here, here + 2)
                elif piece == side:
                    text_send(side, 3, piece, here, 7)
        if pieces[-1] == 0:
            return
        if d < 4:
            swap(2 * d - 1)
            swap(2 * d)
        else:
            swap(7)

    sharp, off = sharp_ref[0], off_ref[0]
    log2_e = 1.4426950408889634
    sharp2, off2 = sharp * log2_e, off * log2_e

    def logits_block(i, j, diagonal=False):
        ri, rj = slice(i * ROWS, (i + 1) * ROWS), slice(j * ROWS, (j + 1) * ROWS)
        logits = sharp2 * contract(ibuf[ri, :], jbuf[rj, :], ((1,), (1,))) + off2
        if diagonal:
            row = lax.broadcasted_iota(jnp.int32, (ROWS, ROWS), 0)
            col = lax.broadcasted_iota(jnp.int32, (ROWS, ROWS), 1)
            same = jnp.logical_and(row == col + yh * HALF, col < HALF)
            logits = jnp.where(same, -logits, logits)
        grown = jnp.exp2(logits)
        total = 1.0 + grown
        rough = pl.reciprocal(total, approx=True)
        inverse = rough * (2.0 - total * rough)
        coef = grown * inverse
        lost = (grown - (total - 1.0)) * inverse
        lacc[ri, :] += jnp.log(total[:, :HALF] * total[:, HALF:]) + (lost[:, :HALF] + lost[:, HALF:])
        if diagonal:
            coef = jnp.where(same, -coef, coef)
        coef = coef.astype(BF16)
        cbuf[ri, rj] = coef
        ctbuf[rj, ri] = coef.T

    def product(out, left, right, m, k0, k1):
        rows, depth = slice(m * ROWS, (m + 1) * ROWS), slice(k0 * ROWS, k1 * ROWS)
        a = left[rows, depth]
        for n in range(0, WIDTH, 256):
            columns = slice(n, min(n + 256, WIDTH))
            result = contract(a, right[depth, columns], ((1,), (0,)))
            out[rows, columns] = result if k0 == 0 else out[rows, columns] + result

    def image_product(i, j0, j1):
        product(pacc, cbuf, jbuf, i, j0, j1)

    def text_product(j, i0, i1):
        product(tacc, ctbuf, ibuf, j, i0, i1)

    up_hi = lax.rem(y + 1, NY) // 2
    turns = (
        other * 2 * (1 - yh) + core * 2 * up_hi,
        core * (2 * up_hi + 1),
        other * 2 * yh + core * 2 * (1 - up_hi),
        core * (2 * (1 - up_hi) + 1),
    )

    def hand_over(slot):
        for side, q, to in ((0, 2 * yh + 1, y_up1), (1, 2 * (1 - yh) + 1, y_down1)):
            rows = pl.ds(pl.multiple_of(slot * ROWS + q * QUARTER, QUARTER), QUARTER)
            ys[side, slot] = pacc[rows, :].astype(BF16)
            send(ys.at[side, slot], yr.at[side, slot], (yc_s, side, slot), yc_r.at[side, slot], to)

    def handed(slot):
        rows = part_rows(slot, 3)
        for side in (0, 1):
            landed(yr.at[side, slot], yc_r.at[side, slot])
        pacc[rows, :] += yr[0, slot].astype(F32) + yr[1, slot].astype(F32)

    def seat(k):
        return pl.ds(k * QUARTER, QUARTER)

    def part_rows(slot, k):
        return pl.ds(pl.multiple_of(slot * ROWS + turns[k] * QUARTER, QUARTER), QUARTER)

    def far_turn(k):
        pb[0, seat(k), :] = pacc[part_rows(3, k), :].astype(BF16)
        send(pb.at[0, seat(k)], xr1.at[seat(k)], (x1_s, k), x1_r.at[k], x_up if k < 2 else x_down)

    def near_turn(slot, k):
        side = 0 if slot == 2 else 1
        rows = pacc[part_rows(slot, k), :]
        if (k < 2) == (slot == 2):
            landed(xr1.at[seat(k)], x1_r.at[k])
            rows = rows + xr1[seat(k), :].astype(F32)
        pb[1 + side, seat(k), :] = rows.astype(BF16)
        send(
            pb.at[1 + side, seat(k)],
            x2.at[side, seat(k)],
            (x2_s, side, k),
            x2_r.at[side, k],
            x_down if side else x_up,
        )

    def text_over(low, count):
        for slot in range(low, low + count):
            mine = pl.ds(pl.multiple_of(slot * HALF + other * QUARTER, QUARTER), QUARTER)
            ts[slot] = tacc[mine, :].astype(BF16)
        slots = pl.ds(low, count)
        send(ts.at[slots], tr.at[slots], (e_s, low), e_r.at[low], sibling)

    def text_came(low, count):
        landed(tr.at[pl.ds(low, count)], e_r.at[low])

    @on(first)
    def _():
        text_hop(1, (0,))
        pass_near(0, 2, True)
        text_hop(1, (1,))
        pass_near(1, 3, True)
        swapped(1)
        logits_block(0, 0, True)
        pass_near(2, 0, False)
        text_hop(2, (0,))
        text_hop(2, (1,))
        pass_near(3, 1, False)
        swapped(2, 3)
        logits_block(0, 1)
        pass_far(0, 2)
        logits_block(1, 0)
        logits_block(2, 0)
        image_product(0, 0, 2)
        text_hop(3)
        pass_far(1, 3)
        logits_block(1, 1)
        logits_block(2, 1)
        image_product(1, 0, 2)
        logits_block(3, 0)
        image_product(2, 0, 2)
        logits_block(3, 1)
        swapped(4, 5)
        text_hop(4)
        text_product(0, 0, 4)
        logits_block(0, 2)
        text_product(1, 0, 4)
        logits_block(1, 2)
        image_product(3, 0, 2)
        logits_block(2, 2)
        logits_block(3, 2)
        swapped(6, 7)
        logits_block(3, 3)
        text_product(2, 0, 4)
        logits_block(1, 3)
        image_product(3, 2, 4)
        logits_block(2, 3)
        image_product(1, 2, 4)
        logits_block(0, 3)
        text_product(3, 0, 4)
        text_over(6, 2)
        text_over(4, 2)
        text_over(0, 4)
        far_turn(0)
        far_turn(2)
        hand_over(3)
        near_turn(1, 0)
        hand_over(1)
        image_product(2, 2, 4)
        near_turn(2, 2)
        hand_over(2)
        image_product(0, 2, 4)
        hand_over(0)

    @on(second)
    def _():
        text_hop(1)
        images_in(0)
        swapped(1)
        logits_block(0, 0)
        text_hop(2)
        swapped(2, 3)
        logits_block(0, 1)
        text_hop(3)
        swapped(4, 5)
        logits_block(0, 2)
        image_product(0, 0, 3)
        text_hop(4)
        images_in(1, 2)
        logits_block(1, 0)
        logits_block(2, 0)
        logits_block(1, 1)
        text_product(0, 0, 3)
        logits_block(2, 1)
        logits_block(1, 2)
        text_product(1, 0, 3)
        logits_block(2, 2)
        swapped(6, 7)
        logits_block(1, 3)
        text_product(2, 0, 3)
        logits_block(2, 3)
        image_product(1, 0, 4)
        logits_block(0, 3)
        image_product(2, 0, 4)
        text_product(3, 0, 3)
        near_turn(1, 0)
        near_turn(2, 2)
        near_turn(1, 1)
        images_in(3)
        logits_block(3, 3)
        logits_block(3, 2)
        text_product(3, 3, 4)
        logits_block(3, 0)
        logits_block(3, 1)
        text_over(6, 2)
        text_product(2, 3, 4)
        text_over(4, 2)
        text_product(1, 3, 4)
        text_product(0, 3, 4)
        text_over(0, 4)
        image_product(3, 0, 4)
        far_turn(0)
        far_turn(2)
        far_turn(1)
        handed(3)
        far_turn(3)
        handed(2)
        near_turn(2, 3)
        image_product(0, 3, 4)

    ones = jnp.ones((8, HALF), F32)
    for i in range(4):
        ls[i] = lax.dot_general(
            ones,
            lacc[i * ROWS : (i + 1) * ROWS, :],
            (((1,), (1,)), ((), ())),
            precision=lax.Precision.HIGHEST,
            preferred_element_type=F32,
        )
    send(ls.at[2], lx.at[0], (lx_s, 0), lx_r.at[0], x_up)
    send(ls.at[1], lx.at[1], (lx_s, 1), lx_r.at[1], x_down)
    send(ls.at[3], lx.at[2], (lx_s, 2), lx_r.at[2], x_far)

    def piece_rows(piece):
        return pl.ds(piece * EIGHTH, EIGHTH)

    def text_sum(slot, piece):
        start = slot * HALF + core * QUARTER + piece * EIGHTH
        return tacc[pl.ds(pl.multiple_of(start, EIGHTH), EIGHTH), :] + tr[slot, piece_rows(piece), :].astype(F32)

    def text_back(d, steps=(0, 1)):
        for step in steps:
            for side in (0, 1):
                piece = step if side else 1 - step
                if d == 4 and piece != side:
                    continue
                rows = text_sum(7 if d == 4 else 2 * d - 1 + side, piece)
                part = piece_rows(piece)
                if d < 3 or (d == 3 and piece == side):
                    landed(vr.at[side, d, part], v_r.at[side, d, piece])
                    rows = rows + vr[side, d, part, :].astype(F32)
                vs[side, d - 1, part, :] = rows.astype(BF16)
                send(
                    vs.at[side, d - 1, part],
                    vr.at[side, d - 1, part],
                    (v_s, side, d - 1, piece),
                    v_r.at[side, d - 1, piece],
                    z_down if side else z_up,
                )

    text_came(6, 2)
    text_back(4)
    text_came(4, 2)
    text_back(3, (0,))
    near_turn(2, 0)
    near_turn(1, 2)
    text_back(3, (1,))
    text_came(0, 4)
    text_back(2, (0,))

    @on(second)
    def _():
        near_turn(2, 1)
        handed(1)
        near_turn(1, 3)

    text_back(2, (1,))
    text_back(1, (0,))

    source = yh + 2 * core
    block_yl = lax.rem(yl + core, 2)

    def owner_of(q):
        to = at(x, 2 * (q // 2) + block_yl, z, q % 2)
        return to, jnp.logical_and(dp == to[0], split == to[1])

    for k in range(3):
        landed(lx.at[k], lx_r.at[k])
    rl[...] = ls[0] + lx[0] + lx[1] + lx[2]
    for q in range(4):
        to, own = owner_of(q)
        send_when(jnp.logical_not(own), (rl, lq.at[source], (ly_s, q), ly_r.at[source], to))

        @pl.when(own)
        def _():
            lq[source] = rl[...]

    text_back(1, (1,))
    drain((i_s, t_s, d_s))

    y_up0, y_down0 = at(x, y + 1, z, 0), at(x, y + 3, z, 0)

    def image_sum(k):
        landed(x2.at[0, seat(k)], x2_r.at[0, k])
        landed(x2.at[1, seat(k)], x2_r.at[1, k])
        return pacc[part_rows(0, k), :] + (x2[0, seat(k), :].astype(F32) + x2[1, seat(k), :].astype(F32))

    def image_out(k, box, to):
        total = image_sum(k)
        if core_of[0] == 1 and k == 0:
            landed(qr.at[3], y_r.at[3])
            total = total + qr[3].astype(F32)
        rb[seat(k), :] = total.astype(BF16)
        send(rb.at[seat(k)], qr.at[box], (y_s, k), y_r.at[box], to)

    core_of = [0]

    @on(first)
    def _():
        image_out(0, 3, y_up1)
        qr[0] = image_sum(2).astype(BF16)

    core_of[0] = 1

    @on(second)
    def _():
        qr[0] = jnp.zeros((QUARTER, WIDTH), BF16)
        image_out(2, 2, y_down0)
        image_out(0, 1, y_up0)

    mine = yh * 2 + core
    outs = (both_out.at[pl.ds(0, ROWS)], both_out.at[pl.ds(ROWS, ROWS)])

    def quarter_rows(q, start=0, count=QUARTER):
        return pl.ds(pl.multiple_of(q * QUARTER + start, EIGHTH), count)

    my_rows = quarter_rows(mine)
    y_up, y_down = at(x, y + 1, z, core), at(x, y + 3, z, core)

    def gather_out(kind, grad, values):
        inverse, unit = unit_rows(values)
        out = outs[kind]
        out[my_rows, :] = unit_back(unit, inverse, sharp * grad).astype(BF16)
        low, high = out.at[quarter_rows(mine, 0, EIGHTH)], out.at[quarter_rows(mine, EIGHTH, EIGHTH)]
        send(low, hop.at[kind, 0], (g_s, kind, 0), g_r.at[kind, 0], y_up)
        send(high, hop.at[kind, 1], (g_s, kind, 1), g_r.at[kind, 1], y_down)
        send(out.at[my_rows], out.at[my_rows], (g_s, kind, 2), g_r.at[kind, 2], sibling)

    def gather_on(kind):
        out = outs[kind]
        landed(hop.at[kind, 0], g_r.at[kind, 0])
        there = out.at[quarter_rows(2 * (1 - up_hi) + core, 0, EIGHTH)]
        send(hop.at[kind, 0], there, (g_s, kind, 3), g_r.at[kind, 3], y_up)
        landed(hop.at[kind, 1], g_r.at[kind, 1])
        there = out.at[quarter_rows(2 * up_hi + core, EIGHTH, EIGHTH)]
        send(hop.at[kind, 1], there, (g_s, kind, 4), g_r.at[kind, 4], y_down)

    def gather_over(kind):
        for half in (0, 1):
            here = outs[kind].at[quarter_rows((1 - yh) * 2 + core, half * EIGHTH, EIGHTH)]
            landed(here, g_r.at[kind, 3 + half])
            send(here, here, (g_s, kind, 5 + half), g_r.at[kind, 5 + half], sibling)

    def gather_end(kind):
        landed(outs[kind].at[quarter_rows(yh * 2 + other)], g_r.at[kind, 2])
        for half in (0, 1):
            here = outs[kind].at[quarter_rows((1 - yh) * 2 + other, half * EIGHTH, EIGHTH)]
            landed(here, g_r.at[kind, 5 + half])

    grads = []
    for piece in (0, 1):
        grad = text_sum(0, piece)
        for side in (0, 1):
            landed(vr.at[side, 0, piece_rows(piece)], v_r.at[side, 0, piece])
            grad = grad + vr[side, 0, piece_rows(piece), :].astype(F32)
        grads.append(grad)
    grad = jnp.concatenate(grads, axis=0)
    gather_out(1, grad, cap[pl.ds(pl.multiple_of(core * QUARTER, QUARTER), QUARTER), :])

    @on(second)
    def _():
        image_out(1, 1, y_up1)
        handed(0)
        image_out(3, 2, y_down1)

    gather_on(1)

    for k in range(4):
        here = jnp.logical_and(first, yh == k)

        @pl.when(jnp.logical_not(here))
        def _():
            landed(lq.at[k], ly_r.at[k])

    loss_out[...] = ((lq[0] + lq[1]) + (lq[2] + lq[3])) * (1.0 / PAIRS)

    landed(qr.at[1], y_r.at[1])
    landed(qr.at[2], y_r.at[2])
    grad = qr[0].astype(F32) + (qr[1].astype(F32) + qr[2].astype(F32))
    gather_out(0, grad, pic[my_rows, :])
    gather_over(1)
    drain()
    gather_on(0)
    gather_over(0)
    gather_end(1)
    gather_end(0)

    drain()
    for cond, rows, ssem in pending:

        @pl.when(cond)
        def _():
            sent(rows, ssem)


def per_device(picture_vectors, caption_vectors, sharpness_entry, offset_shift):
    dma = pltpu.SemaphoreType.DMA
    vmem = pl.BlockSpec(memory_space=pltpu.VMEM)
    smem = pl.BlockSpec(memory_space=pltpu.SMEM)
    hbm = pl.BlockSpec(memory_space=pltpu.HBM)
    both, loss = pl.pallas_call(
        kernel,
        out_shape=(
            jax.ShapeDtypeStruct((2 * ROWS, WIDTH), BF16),
            jax.ShapeDtypeStruct((8, ROWS), F32),
        ),
        in_specs=[hbm, hbm, smem, smem],
        out_specs=(vmem, vmem),
        scratch_shapes=[
            pltpu.VMEM((ROWS, WIDTH), BF16),
            pltpu.VMEM((HALF, WIDTH), BF16),
            pltpu.VMEM((4 * ROWS, WIDTH), BF16),
            pltpu.VMEM((8 * HALF, WIDTH), BF16),
            pltpu.VMEM((4 * ROWS, 8 * HALF), BF16),
            pltpu.VMEM((8 * HALF, 4 * ROWS), BF16),
            pltpu.VMEM((4 * ROWS, WIDTH), F32),
            pltpu.VMEM((8 * HALF, WIDTH), F32),
            pltpu.VMEM((4 * ROWS, HALF), F32),
            pltpu.VMEM((3, ROWS, WIDTH), BF16),
            pltpu.VMEM((ROWS, WIDTH), BF16),
            pltpu.VMEM((2, ROWS, WIDTH), BF16),
            pltpu.VMEM((ROWS, WIDTH), BF16),
            pltpu.VMEM((4, QUARTER, WIDTH), BF16),
            pltpu.VMEM((2, 4, QUARTER, WIDTH), BF16),
            pltpu.VMEM((2, 4, QUARTER, WIDTH), BF16),
            pltpu.VMEM((8, QUARTER, WIDTH), BF16),
            pltpu.VMEM((8, QUARTER, WIDTH), BF16),
            pltpu.VMEM((2, 4, QUARTER, WIDTH), BF16),
            pltpu.VMEM((2, 4, QUARTER, WIDTH), BF16),
            pltpu.VMEM((4, 8, ROWS), F32),
            pltpu.VMEM((3, 8, ROWS), F32),
            pltpu.VMEM((8, ROWS), F32),
            pltpu.VMEM((4, 8, ROWS), F32),
            pltpu.VMEM((2, 2, EIGHTH, WIDTH), BF16),
            dma((2,)),
            dma((7, 4)), dma((4, 4)),
            dma((2, 4, 2)), dma((2, 4, 2)),
            dma((8,)), dma((8,)),
            dma((4,)), dma((4,)),
            dma((2, 4)), dma((2, 4)),
            dma((4,)), dma((4,)),
            dma((2, 4)), dma((2, 4)),
            dma((4,)), dma((4,)),
            dma((3,)), dma((3,)),
            dma((8,)), dma((8,)),
            dma((2, 4, 2)), dma((2, 4, 2)),
            dma((2, 7)), dma((2, 7)),
        ],
        compiler_params=pltpu.CompilerParams(
            collective_id=0, has_side_effects=True, vmem_limit_bytes=48 * 1024 * 1024
        ),
        cost_estimate=pl.CostEstimate(flops=7_300_000_000, bytes_accessed=4_000_000, transcendentals=3_000_000),
    )(
        pltpu.with_memory_space_constraint(picture_vectors, pltpu.HBM),
        pltpu.with_memory_space_constraint(caption_vectors, pltpu.HBM),
        sharpness_entry,
        offset_shift,
    )
    return both[:ROWS].astype(F32), both[ROWS:].astype(F32), loss[0]


def solution(mesh):
    placed = (P("dp", None), P("dp", None), P(), P())
    return jax.shard_map(
        per_device,
        mesh=mesh,
        in_specs=placed,
        out_specs=(P("dp", None), P("dp", None), P("dp")),
        check_vma=False,
    )
```

time: 79.8 us -> 74.7 us (0.936)
  Pallas kernels: 74.5 us -> 70.5 us
    pallas_call x1, Pallas kernels: 74.5 us -> 70.5 us  [per_device(): pl.pallas_call(kernel, out_shape=(jax.ShapeDtypeStruct((2 * ROWS, WIDTH),...]
    convert_element_type x2 -> x1, other arithmetic: 2.18 us -> 1.56 us  [per_device(): return (both[:ROWS].astype(F32), both[ROWS:].astype(F32), loss[0])]
where the time goes in v3:
time: 74.7 us; the launch traced here: 74.6 us
  Pallas kernels  70.5 us (94%)
  between operations  1.93 us (3%)
  other arithmetic  1.56 us (2%)
    pallas_call x1, Pallas kernels, per_device(): pl.pallas_call(kernel, out_shape=(jax.ShapeDtypeStruct((2 * ROWS, WIDTH),...  70.5 us
    convert_element_type x1, other arithmetic, per_device(): return (both[:ROWS].astype(F32), both[ROWS:].astype(F32), loss[0])  1.56 us

profile of v3, /device:TPU:1, one launch (start us, length us, event | category | flops | bytes accessed | tf_op | source)
XLA Modules:
  0.0 74.6 jit_solution(15520579028782051800)
XLA Ops:
  1.9 70.5 %shard_map.67 = (bf16[512,1152]{1,0:T(8,128)(2,1)S(1)}, f32[8,256]{1,0:T(8,128)S(1)}) custom-call(bf16[256,1152]{1,0:T(8,128)(2,1)} %pic_hbm.1, bf16[256,1152]{1,0:T(8,128)(2,1)} %cap_hbm.1, f32[1]{0:T(128)S(6)} %copy.7.sharp_ref, f32[1]{0:T(128)S(6)} %copy.8.off_ref), custom_call_target="tpu_custom_call" | custom-call | flops 7299999744 | bytes 4000000 | tf_op jit(solution)/shard_map/pallas_call | solution.py:645
  72.4 0.6 slice.11
  73.0 1.6 %slice_convert_fusion = (f32[256,1152]{1,0:T(8,128)}, f32[256,1152]{1,0:T(8,128)}) fusion(bf16[512,1152]{1,0:T(8,128)(2,1)S(1)} %get-tuple-element.5), kind=kLoop, calls=%fused_computation | loop fusion | flops 589824 | bytes 3538944 | tf_op jit(solution)/shard_map/convert_element_type | solution.py:703

commit v4 on v3

--- a/solution.py
+++ b/solution.py
@@ -132,12 +132,6 @@
 
     fetch_text.wait()
     jbuf[0:HALF, :] = unit_rows(cap[...])[1].astype(BF16)
-    fetch_image.wait()
-
-    @pl.when(first)
-    def _():
-        ibuf[0:ROWS, :] = unit_rows(pic[...])[1].astype(BF16)
-
     pl.semaphore_wait(barrier, len(partners))
 
     def irows(slot, piece):
@@ -169,6 +163,12 @@
     def to_x(source, slot, piece, kind):
         target = x_up if slot == 1 or (slot == 3 and piece < 2) else x_down
         return (irows(source, piece), irows(slot, piece), (i_s, kind, piece), i_r.at[slot, piece], target)
+
+    fetch_image.wait()
+
+    @pl.when(first)
+    def _():
+        ibuf[0:ROWS, :] = unit_rows(pic[...])[1].astype(BF16)
 
     send_when(
         first,
@@ -327,6 +327,33 @@
 
     def text_came(low, count):
         landed(tr.at[pl.ds(low, count)], e_r.at[low])
+
+    def piece_rows(piece):
+        return pl.ds(piece * EIGHTH, EIGHTH)
+
+    def text_sum(slot, piece):
+        start = slot * HALF + core * QUARTER + piece * EIGHTH
+        return tacc[pl.ds(pl.multiple_of(start, EIGHTH), EIGHTH), :] + tr[slot, piece_rows(piece), :].astype(F32)
+
+    def text_back(d, steps=(0, 1)):
+        for step in steps:
+            for side in (0, 1):
+                piece = step if side else 1 - step
+                if d == 4 and piece != side:
+                    continue
+                rows = text_sum(7 if d == 4 else 2 * d - 1 + side, piece)
+                part = piece_rows(piece)
+                if d < 3 or (d == 3 and piece == side):
+                    landed(vr.at[side, d, part], v_r.at[side, d, piece])
+                    rows = rows + vr[side, d, part, :].astype(F32)
+                vs[side, d - 1, part, :] = rows.astype(BF16)
+                send(
+                    vs.at[side, d - 1, part],
+                    vr.at[side, d - 1, part],
+                    (v_s, side, d - 1, piece),
+                    v_r.at[side, d - 1, piece],
+                    z_down if side else z_up,
+                )
 
     @on(first)
     def _():
@@ -363,18 +390,18 @@
         image_product(3, 0, 2)
         logits_block(2, 2)
         logits_block(3, 2)
+        text_product(2, 0, 4)
+        text_over(0, 4)
+        text_over(4, 2)
         swapped(6, 7)
         logits_block(3, 3)
-        text_product(2, 0, 4)
         logits_block(1, 3)
         image_product(3, 2, 4)
         logits_block(2, 3)
-        image_product(1, 2, 4)
         logits_block(0, 3)
         text_product(3, 0, 4)
         text_over(6, 2)
-        text_over(4, 2)
-        text_over(0, 4)
+        image_product(1, 2, 4)
         far_turn(0)
         far_turn(2)
         hand_over(3)
@@ -385,6 +412,10 @@
         hand_over(2)
         image_product(0, 2, 4)
         hand_over(0)
+        text_came(6, 2)
+        text_back(4)
+        text_came(4, 2)
+        text_back(3, (0,))
 
     @on(second)
     def _():
@@ -424,23 +455,31 @@
         logits_block(3, 3)
         logits_block(3, 2)
         text_product(3, 3, 4)
-        logits_block(3, 0)
+        text_over(6, 2)
         logits_block(3, 1)
-        text_over(6, 2)
         text_product(2, 3, 4)
         text_over(4, 2)
+        logits_block(3, 0)
         text_product(1, 3, 4)
+        text_came(6, 2)
+        text_back(4)
         text_product(0, 3, 4)
         text_over(0, 4)
         image_product(3, 0, 4)
         far_turn(0)
         far_turn(2)
         far_turn(1)
+        text_came(4, 2)
+        text_back(3, (0,))
         handed(3)
         far_turn(3)
         handed(2)
         near_turn(2, 3)
         image_product(0, 3, 4)
+
+    near_turn(2, 0)
+    near_turn(1, 2)
+    text_back(3, (1,))
 
     ones = jnp.ones((8, HALF), F32)
     for i in range(4):
@@ -455,40 +494,6 @@
     send(ls.at[1], lx.at[1], (lx_s, 1), lx_r.at[1], x_down)
     send(ls.at[3], lx.at[2], (lx_s, 2), lx_r.at[2], x_far)
 
-    def piece_rows(piece):
-        return pl.ds(piece * EIGHTH, EIGHTH)
-
-    def text_sum(slot, piece):
-        start = slot * HALF + core * QUARTER + piece * EIGHTH
-        return tacc[pl.ds(pl.multiple_of(start, EIGHTH), EIGHTH), :] + tr[slot, piece_rows(piece), :].astype(F32)
-
-    def text_back(d, steps=(0, 1)):
-        for step in steps:
-            for side in (0, 1):
-                piece = step if side else 1 - step
-                if d == 4 and piece != side:
-                    continue
-                rows = text_sum(7 if d == 4 else 2 * d - 1 + side, piece)
-                part = piece_rows(piece)
-                if d < 3 or (d == 3 and piece == side):
-                    landed(vr.at[side, d, part], v_r.at[side, d, piece])
-                    rows = rows + vr[side, d, part, :].astype(F32)
-                vs[side, d - 1, part, :] = rows.astype(BF16)
-                send(
-                    vs.at[side, d - 1, part],
-                    vr.at[side, d - 1, part],
-                    (v_s, side, d - 1, piece),
-                    v_r.at[side, d - 1, piece],
-                    z_down if side else z_up,
-                )
-
-    text_came(6, 2)
-    text_back(4)
-    text_came(4, 2)
-    text_back(3, (0,))
-    near_turn(2, 0)
-    near_turn(1, 2)
-    text_back(3, (1,))
     text_came(0, 4)
     text_back(2, (0,))
 

time: 74.7 us -> 73 us (0.977)
  Pallas kernels: 70.5 us -> 68.8 us
    pallas_call x1, Pallas kernels: 70.5 us -> 68.8 us  [per_device(): pl.pallas_call(kernel, out_shape=(jax.ShapeDtypeStruct((2 * ROWS, WIDTH),...]
where the time goes in v4:
time: 73 us; the launch traced here: 72.9 us
  Pallas kernels  68.8 us (94%)
  between operations  1.93 us (3%)
  other arithmetic  1.56 us (2%)
    pallas_call x1, Pallas kernels, per_device(): pl.pallas_call(kernel, out_shape=(jax.ShapeDtypeStruct((2 * ROWS, WIDTH),...  68.8 us
    convert_element_type x1, other arithmetic, per_device(): return (both[:ROWS].astype(F32), both[ROWS:].astype(F32), loss[0])  1.56 us

profile of v4, /device:TPU:1, one launch (start us, length us, event | category | flops | bytes accessed | tf_op | source)
XLA Modules:
  0.0 72.9 jit_solution(9888477120168377914)
XLA Ops:
  1.9 68.8 %shard_map.67 = (bf16[512,1152]{1,0:T(8,128)(2,1)S(1)}, f32[8,256]{1,0:T(8,128)S(1)}) custom-call(bf16[256,1152]{1,0:T(8,128)(2,1)} %pic_hbm.1, bf16[256,1152]{1,0:T(8,128)(2,1)} %cap_hbm.1, f32[1]{0:T(128)S(6)} %copy.7.sharp_ref, f32[1]{0:T(128)S(6)} %copy.8.off_ref), custom_call_target="tpu_custom_call" | custom-call | flops 7299999744 | bytes 4000000 | tf_op jit(solution)/shard_map/pallas_call | solution.py:650
  70.7 0.6 slice.11
  71.3 1.6 %slice_convert_fusion = (f32[256,1152]{1,0:T(8,128)}, f32[256,1152]{1,0:T(8,128)}) fusion(bf16[512,1152]{1,0:T(8,128)(2,1)S(1)} %get-tuple-element.5), kind=kLoop, calls=%fused_computation | loop fusion | flops 589824 | bytes 3538944 | tf_op jit(solution)/shard_map/convert_element_type | solution.py:708

commit v5 on v4

--- a/solution.py
+++ b/solution.py
@@ -397,14 +397,14 @@
         logits_block(3, 3)
         logits_block(1, 3)
         image_product(3, 2, 4)
+        far_turn(0)
+        far_turn(2)
+        hand_over(3)
         logits_block(2, 3)
         logits_block(0, 3)
         text_product(3, 0, 4)
         text_over(6, 2)
         image_product(1, 2, 4)
-        far_turn(0)
-        far_turn(2)
-        hand_over(3)
         near_turn(1, 0)
         hand_over(1)
         image_product(2, 2, 4)
@@ -455,24 +455,24 @@
         logits_block(3, 3)
         logits_block(3, 2)
         text_product(3, 3, 4)
+        logits_block(3, 1)
         text_over(6, 2)
-        logits_block(3, 1)
-        text_product(2, 3, 4)
-        text_over(4, 2)
         logits_block(3, 0)
-        text_product(1, 3, 4)
-        text_came(6, 2)
-        text_back(4)
-        text_product(0, 3, 4)
-        text_over(0, 4)
         image_product(3, 0, 4)
         far_turn(0)
         far_turn(2)
         far_turn(1)
+        text_came(6, 2)
+        text_back(4)
+        text_product(2, 3, 4)
+        text_over(4, 2)
+        text_product(1, 3, 4)
+        text_product(0, 3, 4)
+        text_over(0, 4)
+        handed(3)
+        far_turn(3)
         text_came(4, 2)
         text_back(3, (0,))
-        handed(3)
-        far_turn(3)
         handed(2)
         near_turn(2, 3)
         image_product(0, 3, 4)
@@ -506,27 +506,6 @@
     text_back(2, (1,))
     text_back(1, (0,))
 
-    source = yh + 2 * core
-    block_yl = lax.rem(yl + core, 2)
-
-    def owner_of(q):
-        to = at(x, 2 * (q // 2) + block_yl, z, q % 2)
-        return to, jnp.logical_and(dp == to[0], split == to[1])
-
-    for k in range(3):
-        landed(lx.at[k], lx_r.at[k])
-    rl[...] = ls[0] + lx[0] + lx[1] + lx[2]
-    for q in range(4):
-        to, own = owner_of(q)
-        send_when(jnp.logical_not(own), (rl, lq.at[source], (ly_s, q), ly_r.at[source], to))
-
-        @pl.when(own)
-        def _():
-            lq[source] = rl[...]
-
-    text_back(1, (1,))
-    drain((i_s, t_s, d_s))
-
     y_up0, y_down0 = at(x, y + 1, z, 0), at(x, y + 3, z, 0)
 
     def image_sum(k):
@@ -547,16 +526,43 @@
     @on(first)
     def _():
         image_out(0, 3, y_up1)
+
+    core_of[0] = 1
+
+    @on(second)
+    def _():
+        image_out(2, 2, y_down0)
+
+    text_back(1, (1,))
+
+    @on(first)
+    def _():
         qr[0] = image_sum(2).astype(BF16)
 
-    core_of[0] = 1
-
     @on(second)
     def _():
         qr[0] = jnp.zeros((QUARTER, WIDTH), BF16)
-        image_out(2, 2, y_down0)
         image_out(0, 1, y_up0)
 
+    source = yh + 2 * core
+    block_yl = lax.rem(yl + core, 2)
+
+    def owner_of(q):
+        to = at(x, 2 * (q // 2) + block_yl, z, q % 2)
+        return to, jnp.logical_and(dp == to[0], split == to[1])
+
+    for k in range(3):
+        landed(lx.at[k], lx_r.at[k])
+    rl[...] = ls[0] + lx[0] + lx[1] + lx[2]
+    for q in range(4):
+        to, own = owner_of(q)
+        send_when(jnp.logical_not(own), (rl, lq.at[source], (ly_s, q), ly_r.at[source], to))
+
+        @pl.when(own)
+        def _():
+            lq[source] = rl[...]
+
+    drain((i_s, t_s, d_s))
     mine = yh * 2 + core
     outs = (both_out.at[pl.ds(0, ROWS)], both_out.at[pl.ds(ROWS, ROWS)])
 

time: 73 us -> 71.5 us (0.979)
  Pallas kernels: 68.8 us -> 67.4 us
    pallas_call x1, Pallas kernels: 68.8 us -> 67.4 us  [per_device(): pl.pallas_call(kernel, out_shape=(jax.ShapeDtypeStruct((2 * ROWS, WIDTH),...]
where the time goes in v5:
time: 71.5 us; the launch traced here: 71.4 us
  Pallas kernels  67.4 us (94%)
  between operations  1.93 us (3%)
  other arithmetic  1.56 us (2%)
    pallas_call x1, Pallas kernels, per_device(): pl.pallas_call(kernel, out_shape=(jax.ShapeDtypeStruct((2 * ROWS, WIDTH),...  67.4 us
    convert_element_type x1, other arithmetic, per_device(): return (both[:ROWS].astype(F32), both[ROWS:].astype(F32), loss[0])  1.56 us

profile of v5, /device:TPU:1, one launch (start us, length us, event | category | flops | bytes accessed | tf_op | source)
XLA Modules:
  0.0 71.4 jit_solution(10496750530131003239)
XLA Ops:
  1.9 67.4 %shard_map.67 = (bf16[512,1152]{1,0:T(8,128)(2,1)S(1)}, f32[8,256]{1,0:T(8,128)S(1)}) custom-call(bf16[256,1152]{1,0:T(8,128)(2,1)} %pic_hbm.1, bf16[256,1152]{1,0:T(8,128)(2,1)} %cap_hbm.1, f32[1]{0:T(128)S(6)} %copy.7.sharp_ref, f32[1]{0:T(128)S(6)} %copy.8.off_ref), custom_call_target="tpu_custom_call" | custom-call | flops 7299999744 | bytes 4000000 | tf_op jit(solution)/shard_map/pallas_call | solution.py:656
  69.3 0.6 slice.11
  69.9 1.6 %slice_convert_fusion = (f32[256,1152]{1,0:T(8,128)}, f32[256,1152]{1,0:T(8,128)}) fusion(bf16[512,1152]{1,0:T(8,128)(2,1)S(1)} %get-tuple-element.5), kind=kLoop, calls=%fused_computation | loop fusion | flops 589824 | bytes 3538944 | tf_op jit(solution)/shard_map/convert_element_type | solution.py:714

commit v6 on v5

--- a/solution.py
+++ b/solution.py
@@ -187,15 +187,14 @@
             send(*to_x(2, 3, down, 6))
         send(*to_y(2, down))
 
-    def pass_far(*pieces):
-        for piece in pieces:
+    def pass_far():
+        for piece in (0, 2):
             landed(irows(3, piece), i_r.at[3, piece])
             send(*to_y(3, piece))
 
-    def images_in(*slots):
-        for slot in slots:
-            for piece in range(4):
-                landed(irows(slot, piece), i_r.at[slot, piece])
+    def images_in(slot, *pieces):
+        for piece in pieces or range(4):
+            landed(irows(slot, piece), i_r.at[slot, piece])
 
     for zeroed in (lacc,):
 
@@ -369,12 +368,12 @@
         pass_near(3, 1, False)
         swapped(2, 3)
         logits_block(0, 1)
-        pass_far(0, 2)
+        pass_far()
         logits_block(1, 0)
         logits_block(2, 0)
         image_product(0, 0, 2)
         text_hop(3)
-        pass_far(1, 3)
+        images_in(3, 1, 3)
         logits_block(1, 1)
         logits_block(2, 1)
         image_product(1, 0, 2)
@@ -399,17 +398,17 @@
         image_product(3, 2, 4)
         far_turn(0)
         far_turn(2)
-        hand_over(3)
         logits_block(2, 3)
-        logits_block(0, 3)
-        text_product(3, 0, 4)
-        text_over(6, 2)
         image_product(1, 2, 4)
         near_turn(1, 0)
+        hand_over(3)
         hand_over(1)
         image_product(2, 2, 4)
         near_turn(2, 2)
+        logits_block(0, 3)
         hand_over(2)
+        text_product(3, 0, 4)
+        text_over(6, 2)
         image_product(0, 2, 4)
         hand_over(0)
         text_came(6, 2)
@@ -426,12 +425,17 @@
         text_hop(2)
         swapped(2, 3)
         logits_block(0, 1)
+        images_in(1, 1)
+        send(*to_x(1, 3, 1, 6))
+        images_in(2, 3)
+        send(*to_x(2, 3, 3, 6))
         text_hop(3)
         swapped(4, 5)
         logits_block(0, 2)
         image_product(0, 0, 3)
         text_hop(4)
-        images_in(1, 2)
+        images_in(1, 0, 2, 3)
+        images_in(2, 0, 1, 2)
         logits_block(1, 0)
         logits_block(2, 0)
         logits_block(1, 1)

time: 71.5 us -> 72.7 us (1.017)
  Pallas kernels: 67.4 us -> 68.5 us
    pallas_call x1, Pallas kernels: 67.4 us -> 68.5 us  [per_device(): pl.pallas_call(kernel, out_shape=(jax.ShapeDtypeStruct((2 * ROWS, WIDTH),...]
where the time goes in v6:
time: 72.7 us; the launch traced here: 72.6 us
  Pallas kernels  68.5 us (94%)
  between operations  1.93 us (3%)
  other arithmetic  1.56 us (2%)
    pallas_call x1, Pallas kernels, per_device(): pl.pallas_call(kernel, out_shape=(jax.ShapeDtypeStruct((2 * ROWS, WIDTH),...  68.5 us
    convert_element_type x1, other arithmetic, per_device(): return (both[:ROWS].astype(F32), both[ROWS:].astype(F32), loss[0])  1.56 us

profile of v6, /device:TPU:1, one launch (start us, length us, event | category | flops | bytes accessed | tf_op | source)
XLA Modules:
  0.0 72.6 jit_solution(4605565083816497533)
XLA Ops:
  1.9 68.5 %shard_map.67 = (bf16[512,1152]{1,0:T(8,128)(2,1)S(1)}, f32[8,256]{1,0:T(8,128)S(1)}) custom-call(bf16[256,1152]{1,0:T(8,128)(2,1)} %pic_hbm.1, bf16[256,1152]{1,0:T(8,128)(2,1)} %cap_hbm.1, f32[1]{0:T(128)S(6)} %copy.7.sharp_ref, f32[1]{0:T(128)S(6)} %copy.8.off_ref), custom_call_target="tpu_custom_call" | custom-call | flops 7299999744 | bytes 4000000 | tf_op jit(solution)/shard_map/pallas_call | solution.py:660
  70.5 0.6 slice.11
  71.0 1.6 %slice_convert_fusion = (f32[256,1152]{1,0:T(8,128)}, f32[256,1152]{1,0:T(8,128)}) fusion(bf16[512,1152]{1,0:T(8,128)(2,1)S(1)} %get-tuple-element.5), kind=kLoop, calls=%fused_computation | loop fusion | flops 589824 | bytes 3538944 | tf_op jit(solution)/shard_map/convert_element_type | solution.py:718

commit v7 on v5

--- a/solution.py
+++ b/solution.py
@@ -11,7 +11,7 @@
 
 NX, NY, NZ = 4, 4, 8
 ROWS, WIDTH = 256, 1152
-HALF, QUARTER, EIGHTH = 128, 64, 32
+HALF, QUARTER, EIGHTH, PIECE = 128, 64, 32, 16
 PAIRS = 16384
 
 
@@ -138,10 +138,10 @@
         return ibuf.at[pl.ds(slot * ROWS + piece * QUARTER, QUARTER)]
 
     def jrows(slot, c, start=0, count=QUARTER):
-        return jbuf.at[pl.ds(pl.multiple_of(slot * HALF + c * QUARTER + start, EIGHTH), count)]
+        return jbuf.at[pl.ds(pl.multiple_of(slot * HALF + c * QUARTER + start, PIECE), count)]
 
     def text_piece(slot, piece):
-        return jrows(slot, core, piece * EIGHTH, EIGHTH)
+        return jrows(slot, core, piece * PIECE, PIECE)
 
     def text_send(side, d, piece, source, target):
         send(
@@ -152,7 +152,7 @@
             z_down if side else z_up,
         )
 
-    for piece in (0, 1):
+    for piece in range(4):
         text_send(0, 0, piece, 0, 2)
         text_send(1, 0, piece, 0, 1)
 
@@ -213,20 +213,20 @@
         for slot in slots:
             landed(jrows(slot, other), d_r.at[slot])
 
-    def text_hop(d, pieces=(0, 1)):
+    def text_hop(d, pieces=(0, 1, 2, 3)):
         for piece in pieces:
             for side in (0, 1):
                 if d == 4:
-                    if piece == side:
+                    if piece // 2 == side:
                         landed(text_piece(7, piece), t_r.at[side, 3, piece])
                     continue
                 here = 2 * d - side
                 landed(text_piece(here, piece), t_r.at[side, d - 1, piece])
                 if d < 3:
                     text_send(side, d, piece, here, here + 2)
-                elif piece == side:
+                elif piece // 2 == side:
                     text_send(side, 3, piece, here, 7)
-        if pieces[-1] == 0:
+        if pieces[-1] != 3:
             return
         if d < 4:
             swap(2 * d - 1)
@@ -329,21 +329,21 @@
         landed(tr.at[pl.ds(low, count)], e_r.at[low])
 
     def piece_rows(piece):
-        return pl.ds(piece * EIGHTH, EIGHTH)
+        return pl.ds(piece * PIECE, PIECE)
 
     def text_sum(slot, piece):
-        start = slot * HALF + core * QUARTER + piece * EIGHTH
-        return tacc[pl.ds(pl.multiple_of(start, EIGHTH), EIGHTH), :] + tr[slot, piece_rows(piece), :].astype(F32)
-
-    def text_back(d, steps=(0, 1)):
+        start = slot * HALF + core * QUARTER + piece * PIECE
+        return tacc[pl.ds(pl.multiple_of(start, PIECE), PIECE), :] + tr[slot, piece_rows(piece), :].astype(F32)
+
+    def text_back(d, steps=(0, 1, 2, 3)):
         for step in steps:
             for side in (0, 1):
-                piece = step if side else 1 - step
-                if d == 4 and piece != side:
+                piece = step if side else (step + 2) % 4
+                if d == 4 and step < 2:
                     continue
                 rows = text_sum(7 if d == 4 else 2 * d - 1 + side, piece)
                 part = piece_rows(piece)
-                if d < 3 or (d == 3 and piece == side):
+                if d < 3 or (d == 3 and step >= 2):
                     landed(vr.at[side, d, part], v_r.at[side, d, piece])
                     rows = rows + vr[side, d, part, :].astype(F32)
                 vs[side, d - 1, part, :] = rows.astype(BF16)
@@ -357,15 +357,14 @@
 
     @on(first)
     def _():
-        text_hop(1, (0,))
+        text_hop(1, (0, 1))
         pass_near(0, 2, True)
-        text_hop(1, (1,))
+        text_hop(1, (2, 3))
         pass_near(1, 3, True)
         swapped(1)
         logits_block(0, 0, True)
         pass_near(2, 0, False)
-        text_hop(2, (0,))
-        text_hop(2, (1,))
+        text_hop(2)
         pass_near(3, 1, False)
         swapped(2, 3)
         logits_block(0, 1)
@@ -415,7 +414,7 @@
         text_came(6, 2)
         text_back(4)
         text_came(4, 2)
-        text_back(3, (0,))
+        text_back(3, (0, 1))
 
     @on(second)
     def _():
@@ -472,14 +471,14 @@
         handed(3)
         far_turn(3)
         text_came(4, 2)
-        text_back(3, (0,))
+        text_back(3, (0, 1))
         handed(2)
         near_turn(2, 3)
         image_product(0, 3, 4)
 
     near_turn(2, 0)
     near_turn(1, 2)
-    text_back(3, (1,))
+    text_back(3, (2, 3))
 
     ones = jnp.ones((8, HALF), F32)
     for i in range(4):
@@ -495,7 +494,7 @@
     send(ls.at[3], lx.at[2], (lx_s, 2), lx_r.at[2], x_far)
 
     text_came(0, 4)
-    text_back(2, (0,))
+    text_back(2, (0, 1))
 
     @on(second)
     def _():
@@ -503,8 +502,8 @@
         handed(1)
         near_turn(1, 3)
 
-    text_back(2, (1,))
-    text_back(1, (0,))
+    text_back(2, (2, 3))
+    text_back(1, (0, 1))
 
     y_up0, y_down0 = at(x, y + 1, z, 0), at(x, y + 3, z, 0)
 
@@ -533,7 +532,7 @@
     def _():
         image_out(2, 2, y_down0)
 
-    text_back(1, (1,))
+    text_back(1, (2, 3))
 
     @on(first)
     def _():
@@ -603,7 +602,7 @@
             landed(here, g_r.at[kind, 5 + half])
 
     grads = []
-    for piece in (0, 1):
+    for piece in range(4):
         grad = text_sum(0, piece)
         for side in (0, 1):
             landed(vr.at[side, 0, piece_rows(piece)], v_r.at[side, 0, piece])
@@ -689,7 +688,7 @@
             pltpu.VMEM((2, 2, EIGHTH, WIDTH), BF16),
             dma((2,)),
             dma((7, 4)), dma((4, 4)),
-            dma((2, 4, 2)), dma((2, 4, 2)),
+            dma((2, 4, 4)), dma((2, 4, 4)),
             dma((8,)), dma((8,)),
             dma((4,)), dma((4,)),
             dma((2, 4)), dma((2, 4)),
@@ -698,7 +697,7 @@
             dma((4,)), dma((4,)),
             dma((3,)), dma((3,)),
             dma((8,)), dma((8,)),
-            dma((2, 4, 2)), dma((2, 4, 2)),
+            dma((2, 4, 4)), dma((2, 4, 4)),
             dma((2, 7)), dma((2, 7)),
         ],
         compiler_params=pltpu.CompilerParams(

time: 71.5 us -> 72.9 us (1.020)
  Pallas kernels: 67.4 us -> 68.8 us
    pallas_call x1, Pallas kernels: 67.4 us -> 68.8 us  [per_device(): pl.pallas_call(kernel, out_shape=(jax.ShapeDtypeStruct((2 * ROWS, WIDTH),...]
where the time goes in v7:
time: 72.9 us; the launch traced here: 72.8 us
  Pallas kernels  68.8 us (94%)
  between operations  1.93 us (3%)
  other arithmetic  1.56 us (2%)
    pallas_call x1, Pallas kernels, per_device(): pl.pallas_call(kernel, out_shape=(jax.ShapeDtypeStruct((2 * ROWS, WIDTH),...  68.8 us
    convert_element_type x1, other arithmetic, per_device(): return (both[:ROWS].astype(F32), both[ROWS:].astype(F32), loss[0])  1.56 us

profile of v7, /device:TPU:1, one launch (start us, length us, event | category | flops | bytes accessed | tf_op | source)
XLA Modules:
  0.0 72.8 jit_solution(2481566045933149792)
XLA Ops:
  1.9 68.8 %shard_map.67 = (bf16[512,1152]{1,0:T(8,128)(2,1)S(1)}, f32[8,256]{1,0:T(8,128)S(1)}) custom-call(bf16[256,1152]{1,0:T(8,128)(2,1)} %pic_hbm.1, bf16[256,1152]{1,0:T(8,128)(2,1)} %cap_hbm.1, f32[1]{0:T(128)S(6)} %copy.7.sharp_ref, f32[1]{0:T(128)S(6)} %copy.8.off_ref), custom_call_target="tpu_custom_call" | custom-call | flops 7299999744 | bytes 4000000 | tf_op jit(solution)/shard_map/pallas_call | solution.py:655
  70.7 0.6 slice.11
  71.3 1.6 %slice_convert_fusion = (f32[256,1152]{1,0:T(8,128)}, f32[256,1152]{1,0:T(8,128)}) fusion(bf16[512,1152]{1,0:T(8,128)(2,1)S(1)} %get-tuple-element.5), kind=kLoop, calls=%fused_computation | loop fusion | flops 589824 | bytes 3538944 | tf_op jit(solution)/shard_map/convert_element_type | solution.py:713

commit v8 on v5

--- a/solution.py
+++ b/solution.py
@@ -192,10 +192,9 @@
             landed(irows(3, piece), i_r.at[3, piece])
             send(*to_y(3, piece))
 
-    def images_in(*slots):
-        for slot in slots:
-            for piece in range(4):
-                landed(irows(slot, piece), i_r.at[slot, piece])
+    def images_in(slot, *pieces):
+        for piece in pieces or range(4):
+            landed(irows(slot, piece), i_r.at[slot, piece])
 
     for zeroed in (lacc,):
 
@@ -238,8 +237,10 @@
     log2_e = 1.4426950408889634
     sharp2, off2 = sharp * log2_e, off * log2_e
 
-    def logits_block(i, j, diagonal=False):
-        ri, rj = slice(i * ROWS, (i + 1) * ROWS), slice(j * ROWS, (j + 1) * ROWS)
+    def logits_block(i, j, diagonal=False, half=None):
+        start = i * ROWS + (half or 0) * HALF
+        ri = slice(start, start + (ROWS if half is None else HALF))
+        rj = slice(j * ROWS, (j + 1) * ROWS)
         logits = sharp2 * contract(ibuf[ri, :], jbuf[rj, :], ((1,), (1,))) + off2
         if diagonal:
             row = lax.broadcasted_iota(jnp.int32, (ROWS, ROWS), 0)
@@ -426,20 +427,29 @@
         text_hop(2)
         swapped(2, 3)
         logits_block(0, 1)
+        images_in(1, 0, 1)
+        images_in(2, 2, 3)
+        logits_block(1, 0, half=0)
+        logits_block(2, 0, half=1)
         text_hop(3)
+        logits_block(1, 1, half=0)
+        logits_block(2, 1, half=1)
         swapped(4, 5)
         logits_block(0, 2)
         image_product(0, 0, 3)
+        logits_block(1, 2, half=0)
+        logits_block(2, 2, half=1)
         text_hop(4)
-        images_in(1, 2)
-        logits_block(1, 0)
-        logits_block(2, 0)
-        logits_block(1, 1)
+        images_in(1, 2, 3)
+        images_in(2, 0, 1)
+        logits_block(1, 0, half=1)
+        logits_block(2, 0, half=0)
+        logits_block(1, 1, half=1)
         text_product(0, 0, 3)
-        logits_block(2, 1)
-        logits_block(1, 2)
+        logits_block(2, 1, half=0)
+        logits_block(1, 2, half=1)
         text_product(1, 0, 3)
-        logits_block(2, 2)
+        logits_block(2, 2, half=0)
         swapped(6, 7)
         logits_block(1, 3)
         text_product(2, 0, 3)
@@ -629,23 +639,25 @@
 
     loss_out[...] = ((lq[0] + lq[1]) + (lq[2] + lq[3])) * (1.0 / PAIRS)
 
+    drain((e_s, v_s, x1_s, x2_s, yc_s, lx_s))
     landed(qr.at[1], y_r.at[1])
     landed(qr.at[2], y_r.at[2])
     grad = qr[0].astype(F32) + (qr[1].astype(F32) + qr[2].astype(F32))
     gather_out(0, grad, pic[my_rows, :])
     gather_over(1)
-    drain()
     gather_on(0)
-    gather_over(0)
-    gather_end(1)
-    gather_end(0)
-
     drain()
     for cond, rows, ssem in pending:
 
         @pl.when(cond)
         def _():
             sent(rows, ssem)
+
+    pending.clear()
+    gather_end(1)
+    gather_over(0)
+    gather_end(0)
+    drain()
 
 
 def per_device(picture_vectors, caption_vectors, sharpness_entry, offset_shift):

time: 71.5 us -> 71.6 us (level)
  no operation moved by 1% of the time
where the time goes in v8:
time: 71.6 us; the launch traced here: 71.5 us
  Pallas kernels  67.4 us (94%)
  between operations  1.93 us (3%)
  other arithmetic  1.56 us (2%)
    pallas_call x1, Pallas kernels, per_device(): pl.pallas_call(kernel, out_shape=(jax.ShapeDtypeStruct((2 * ROWS, WIDTH),...  67.4 us
    convert_element_type x1, other arithmetic, per_device(): return (both[:ROWS].astype(F32), both[ROWS:].astype(F32), loss[0])  1.56 us

profile of v8, /device:TPU:1, one launch (start us, length us, event | category | flops | bytes accessed | tf_op | source)
XLA Modules:
  0.0 71.5 jit_solution(9450247861504322722)
XLA Ops:
  1.9 67.4 %shard_map.67 = (bf16[512,1152]{1,0:T(8,128)(2,1)S(1)}, f32[8,256]{1,0:T(8,128)S(1)}) custom-call(bf16[256,1152]{1,0:T(8,128)(2,1)} %pic_hbm.1, bf16[256,1152]{1,0:T(8,128)(2,1)} %cap_hbm.1, f32[1]{0:T(128)S(6)} %copy.7.sharp_ref, f32[1]{0:T(128)S(6)} %copy.8.off_ref), custom_call_target="tpu_custom_call" | custom-call | flops 7299999744 | bytes 4000000 | tf_op jit(solution)/shard_map/pallas_call | solution.py:668
  69.3 0.6 slice.11
  69.9 1.6 %slice_convert_fusion = (f32[256,1152]{1,0:T(8,128)}, f32[256,1152]{1,0:T(8,128)}) fusion(bf16[512,1152]{1,0:T(8,128)(2,1)S(1)} %get-tuple-element.5), kind=kLoop, calls=%fused_computation | loop fusion | flops 589824 | bytes 3538944 | tf_op jit(solution)/shard_map/convert_element_type | solution.py:726

commit v9 on v8

--- a/solution.py
+++ b/solution.py
@@ -579,16 +579,19 @@
     def quarter_rows(q, start=0, count=QUARTER):
         return pl.ds(pl.multiple_of(q * QUARTER + start, EIGHTH), count)
 
-    my_rows = quarter_rows(mine)
-    y_up, y_down = at(x, y + 1, z, core), at(x, y + 3, z, core)
+    my_rows, my_other = quarter_rows(mine), quarter_rows(yh * 2 + other)
+    y_up, y_down, y_far = (at(x, y + k, z, core) for k in (1, 3, 2))
 
     def gather_out(kind, grad, values):
         inverse, unit = unit_rows(values)
         out = outs[kind]
         out[my_rows, :] = unit_back(unit, inverse, sharp * grad).astype(BF16)
-        low, high = out.at[quarter_rows(mine, 0, EIGHTH)], out.at[quarter_rows(mine, EIGHTH, EIGHTH)]
-        send(low, hop.at[kind, 0], (g_s, kind, 0), g_r.at[kind, 0], y_up)
-        send(high, hop.at[kind, 1], (g_s, kind, 1), g_r.at[kind, 1], y_down)
+        if kind == 0:
+            send(out.at[my_rows], out.at[my_rows], (g_s, 0, 0), g_r.at[0, 3], y_far)
+        else:
+            low, high = out.at[quarter_rows(mine, 0, EIGHTH)], out.at[quarter_rows(mine, EIGHTH, EIGHTH)]
+            send(low, hop.at[kind, 0], (g_s, kind, 0), g_r.at[kind, 0], y_up)
+            send(high, hop.at[kind, 1], (g_s, kind, 1), g_r.at[kind, 1], y_down)
         send(out.at[my_rows], out.at[my_rows], (g_s, kind, 2), g_r.at[kind, 2], sibling)
 
     def gather_on(kind):
@@ -645,7 +648,6 @@
     grad = qr[0].astype(F32) + (qr[1].astype(F32) + qr[2].astype(F32))
     gather_out(0, grad, pic[my_rows, :])
     gather_over(1)
-    gather_on(0)
     drain()
     for cond, rows, ssem in pending:
 
@@ -655,8 +657,11 @@
 
     pending.clear()
     gather_end(1)
-    gather_over(0)
-    gather_end(0)
+    far_rows, last_rows = quarter_rows((1 - yh) * 2 + core), quarter_rows((1 - yh) * 2 + other)
+    landed(outs[0].at[far_rows], g_r.at[0, 3])
+    send(outs[0].at[far_rows], outs[0].at[far_rows], (g_s, 0, 5), g_r.at[0, 5], sibling)
+    landed(outs[0].at[my_other], g_r.at[0, 2])
+    landed(outs[0].at[last_rows], g_r.at[0, 5])
     drain()
 
 

time: 71.6 us -> 69.9 us (0.976)
  Pallas kernels: 67.4 us -> 65.7 us
    pallas_call x1, Pallas kernels: 67.4 us -> 65.7 us  [per_device(): pl.pallas_call(kernel, out_shape=(jax.ShapeDtypeStruct((2 * ROWS, WIDTH),...]
where the time goes in v9:
time: 69.9 us; the launch traced here: 69.7 us
  Pallas kernels  65.7 us (94%)
  between operations  1.93 us (3%)
  other arithmetic  1.56 us (2%)
    pallas_call x1, Pallas kernels, per_device(): pl.pallas_call(kernel, out_shape=(jax.ShapeDtypeStruct((2 * ROWS, WIDTH),...  65.7 us
    convert_element_type x1, other arithmetic, per_device(): return (both[:ROWS].astype(F32), both[ROWS:].astype(F32), loss[0])  1.56 us

profile of v9, /device:TPU:1, one launch (start us, length us, event | category | flops | bytes accessed | tf_op | source)
XLA Modules:
  0.0 69.7 jit_solution(8717648353982253508)
XLA Ops:
  1.9 65.7 %shard_map.67 = (bf16[512,1152]{1,0:T(8,128)(2,1)S(1)}, f32[8,256]{1,0:T(8,128)S(1)}) custom-call(bf16[256,1152]{1,0:T(8,128)(2,1)} %pic_hbm.1, bf16[256,1152]{1,0:T(8,128)(2,1)} %cap_hbm.1, f32[1]{0:T(128)S(6)} %copy.7.sharp_ref, f32[1]{0:T(128)S(6)} %copy.8.off_ref), custom_call_target="tpu_custom_call" | custom-call | flops 7299999744 | bytes 4000000 | tf_op jit(solution)/shard_map/pallas_call | solution.py:673
  67.6 0.6 slice.11
  68.2 1.6 %slice_convert_fusion = (f32[256,1152]{1,0:T(8,128)}, f32[256,1152]{1,0:T(8,128)}) fusion(bf16[512,1152]{1,0:T(8,128)(2,1)S(1)} %get-tuple-element.5), kind=kLoop, calls=%fused_computation | loop fusion | flops 589824 | bytes 3538944 | tf_op jit(solution)/shard_map/convert_element_type | solution.py:731

commit v10 on v8

--- a/solution.py
+++ b/solution.py
@@ -36,7 +36,6 @@
     pb, xr1, x2, rb, qr, ys, yr,
     ts, tr, vs, vr,
     ls, lx, rl, lq,
-    hop,
     in_sem, i_s, i_r, t_s, t_r, d_s, d_r, x1_s, x1_r, x2_s, x2_r, y_s, y_r, yc_s, yc_r,
     ly_s, ly_r, lx_s, lx_r, e_s, e_r, v_s, v_r, g_s, g_r,
 ):
@@ -525,23 +524,17 @@
 
     def image_out(k, box, to):
         total = image_sum(k)
-        if core_of[0] == 1 and k == 0:
-            landed(qr.at[3], y_r.at[3])
-            total = total + qr[3].astype(F32)
         rb[seat(k), :] = total.astype(BF16)
         send(rb.at[seat(k)], qr.at[box], (y_s, k), y_r.at[box], to)
 
-    core_of = [0]
-
     @on(first)
     def _():
-        image_out(0, 3, y_up1)
-
-    core_of[0] = 1
+        image_out(0, 3, at(x, y + 2, z, 0))
 
     @on(second)
     def _():
         image_out(2, 2, y_down0)
+        image_out(0, 1, y_up0)
 
     text_back(1, (1,))
 
@@ -552,7 +545,7 @@
     @on(second)
     def _():
         qr[0] = jnp.zeros((QUARTER, WIDTH), BF16)
-        image_out(0, 1, y_up0)
+        qr[3] = jnp.zeros((QUARTER, WIDTH), BF16)
 
     source = yh + 2 * core
     block_yl = lax.rem(yl + core, 2)
@@ -579,38 +572,27 @@
     def quarter_rows(q, start=0, count=QUARTER):
         return pl.ds(pl.multiple_of(q * QUARTER + start, EIGHTH), count)
 
-    my_rows = quarter_rows(mine)
-    y_up, y_down = at(x, y + 1, z, core), at(x, y + 3, z, core)
+    my_rows, my_other = quarter_rows(mine), quarter_rows(yh * 2 + other)
+    y_far = at(x, y + 2, z, core)
+
+    far_rows, last_rows = quarter_rows((1 - yh) * 2 + core), quarter_rows((1 - yh) * 2 + other)
 
     def gather_out(kind, grad, values):
         inverse, unit = unit_rows(values)
         out = outs[kind]
         out[my_rows, :] = unit_back(unit, inverse, sharp * grad).astype(BF16)
-        low, high = out.at[quarter_rows(mine, 0, EIGHTH)], out.at[quarter_rows(mine, EIGHTH, EIGHTH)]
-        send(low, hop.at[kind, 0], (g_s, kind, 0), g_r.at[kind, 0], y_up)
-        send(high, hop.at[kind, 1], (g_s, kind, 1), g_r.at[kind, 1], y_down)
-        send(out.at[my_rows], out.at[my_rows], (g_s, kind, 2), g_r.at[kind, 2], sibling)
-
-    def gather_on(kind):
-        out = outs[kind]
-        landed(hop.at[kind, 0], g_r.at[kind, 0])
-        there = out.at[quarter_rows(2 * (1 - up_hi) + core, 0, EIGHTH)]
-        send(hop.at[kind, 0], there, (g_s, kind, 3), g_r.at[kind, 3], y_up)
-        landed(hop.at[kind, 1], g_r.at[kind, 1])
-        there = out.at[quarter_rows(2 * up_hi + core, EIGHTH, EIGHTH)]
-        send(hop.at[kind, 1], there, (g_s, kind, 4), g_r.at[kind, 4], y_down)
+        here = out.at[my_rows]
+        send(here, here, (g_s, kind, 0), g_r.at[kind, 0], y_far)
+        send(here, here, (g_s, kind, 1), g_r.at[kind, 1], sibling)
 
     def gather_over(kind):
-        for half in (0, 1):
-            here = outs[kind].at[quarter_rows((1 - yh) * 2 + core, half * EIGHTH, EIGHTH)]
-            landed(here, g_r.at[kind, 3 + half])
-            send(here, here, (g_s, kind, 5 + half), g_r.at[kind, 5 + half], sibling)
+        here = outs[kind].at[far_rows]
+        landed(here, g_r.at[kind, 0])
+        send(here, here, (g_s, kind, 2), g_r.at[kind, 2], sibling)
 
     def gather_end(kind):
-        landed(outs[kind].at[quarter_rows(yh * 2 + other)], g_r.at[kind, 2])
-        for half in (0, 1):
-            here = outs[kind].at[quarter_rows((1 - yh) * 2 + other, half * EIGHTH, EIGHTH)]
-            landed(here, g_r.at[kind, 5 + half])
+        landed(outs[kind].at[my_other], g_r.at[kind, 1])
+        landed(outs[kind].at[last_rows], g_r.at[kind, 2])
 
     grads = []
     for piece in (0, 1):
@@ -628,8 +610,6 @@
         handed(0)
         image_out(3, 2, y_down1)
 
-    gather_on(1)
-
     for k in range(4):
         here = jnp.logical_and(first, yh == k)
 
@@ -642,10 +622,14 @@
     drain((e_s, v_s, x1_s, x2_s, yc_s, lx_s))
     landed(qr.at[1], y_r.at[1])
     landed(qr.at[2], y_r.at[2])
-    grad = qr[0].astype(F32) + (qr[1].astype(F32) + qr[2].astype(F32))
+
+    @on(first)
+    def _():
+        landed(qr.at[3], y_r.at[3])
+
+    grad = (qr[0].astype(F32) + qr[3].astype(F32)) + (qr[1].astype(F32) + qr[2].astype(F32))
     gather_out(0, grad, pic[my_rows, :])
     gather_over(1)
-    gather_on(0)
     drain()
     for cond, rows, ssem in pending:
 
@@ -654,8 +638,8 @@
             sent(rows, ssem)
 
     pending.clear()
+    gather_over(0)
     gather_end(1)
-    gather_over(0)
     gather_end(0)
     drain()
 
@@ -698,7 +682,6 @@
             pltpu.VMEM((3, 8, ROWS), F32),
             pltpu.VMEM((8, ROWS), F32),
             pltpu.VMEM((4, 8, ROWS), F32),
-            pltpu.VMEM((2, 2, EIGHTH, WIDTH), BF16),
             dma((2,)),
             dma((7, 4)), dma((4, 4)),
             dma((2, 4, 2)), dma((2, 4, 2)),
@@ -711,7 +694,7 @@
             dma((3,)), dma((3,)),
             dma((8,)), dma((8,)),
             dma((2, 4, 2)), dma((2, 4, 2)),
-            dma((2, 7)), dma((2, 7)),
+            dma((2, 3)), dma((2, 3)),
         ],
         compiler_params=pltpu.CompilerParams(
             collective_id=0, has_side_effects=True, vmem_limit_bytes=48 * 1024 * 1024

time: 71.6 us -> 71.4 us (level)
  no operation moved by 1% of the time
where the time goes in v10:
time: 71.4 us; the launch traced here: 71.3 us
  Pallas kernels  67.2 us (94%)
  between operations  1.93 us (3%)
  other arithmetic  1.56 us (2%)
    pallas_call x1, Pallas kernels, per_device(): pl.pallas_call(kernel, out_shape=(jax.ShapeDtypeStruct((2 * ROWS, WIDTH),...  67.2 us
    convert_element_type x1, other arithmetic, per_device(): return (both[:ROWS].astype(F32), both[ROWS:].astype(F32), loss[0])  1.56 us

profile of v10, /device:TPU:1, one launch (start us, length us, event | category | flops | bytes accessed | tf_op | source)
XLA Modules:
  0.0 71.3 jit_solution(10014711436827175072)
XLA Ops:
  1.9 67.2 %shard_map.67 = (bf16[512,1152]{1,0:T(8,128)(2,1)S(1)}, f32[8,256]{1,0:T(8,128)S(1)}) custom-call(bf16[256,1152]{1,0:T(8,128)(2,1)} %pic_hbm.1, bf16[256,1152]{1,0:T(8,128)(2,1)} %cap_hbm.1, f32[1]{0:T(128)S(6)} %copy.7.sharp_ref, f32[1]{0:T(128)S(6)} %copy.8.off_ref), custom_call_target="tpu_custom_call" | custom-call | flops 7299999744 | bytes 4000000 | tf_op jit(solution)/shard_map/pallas_call | solution.py:652
  69.1 0.6 slice.11
  69.7 1.6 %slice_convert_fusion = (f32[256,1152]{1,0:T(8,128)}, f32[256,1152]{1,0:T(8,128)}) fusion(bf16[512,1152]{1,0:T(8,128)(2,1)S(1)} %get-tuple-element.5), kind=kLoop, calls=%fused_computation | loop fusion | flops 589824 | bytes 3538944 | tf_op jit(solution)/shard_map/convert_element_type | solution.py:709
